TPU v7x, 256 devices: a whole 4x4x8 slice. The times are simulated.
256 devices in a mesh: ctx: 16 (over x, z_hi, core), fsdp: 16 (over y, z_lo).
Axes of the slice: x: 4, y: 4, z: 8 (z_hi: 2, z_lo: 4; z = z_hi * 4 + z_lo), core: 2. Of those that a mesh axis runs over, the one named last changes fastest.
Arguments:
- rows_in: bfloat16 [16, 2048, 12288], P('fsdp', 'ctx'), may hold values from -6 to 6
- cotangent: bfloat16 [16, 2048, 4096], P('fsdp', 'ctx'), may hold values from -6 to 6
- taps: float32 [3, 12288], P(None, 'fsdp'), may hold values from -3 to 3
- residues: float32 [16, 4096], P(None, 'fsdp'), may hold values from -1 to 1, as said below
- rates: float32 [16, 4096], P(None, 'fsdp'), may hold values from 0 to 1, as said below
- skip: float32 [4096], P('fsdp'), may hold values from -3 to 3
- state_before: float32 [16, 16, 4096], P('fsdp'), may hold values from -24 to 24
- adjoint_after: float32 [16, 16, 4096], P('fsdp'), may hold values from -24 to 24
Outputs:
- grad_rows: bfloat16 [16, 2048, 12288], P('fsdp', 'ctx')
- grad_taps: float32 [3, 12288], P(None, 'fsdp')
- grad_residues: float32 [16, 4096], P(None, 'fsdp')
- grad_rates: float32 [16, 4096], P(None, 'fsdp')
- grad_skip: float32 [4096], P('fsdp')
Inputs may be any that keep to these rules, and one draw needn't show every extreme that they name: Positive decay rates. Real residues.
All inputs are finite; a program needn't handle non-finite values.
Results may differ from a plain program's by a relative error of at most 0.0011.
Values may be sent and summed in bfloat16 or wider, within the bound.
A program may use at most 128 MiB of HBM per device.

v0:
```python
import jax
import jax.numpy as jnp
from jax import lax
from jax.sharding import PartitionSpec as P

BLOCK = 16


def from_behind(block, axis, distance):
    devices = range(lax.axis_size(axis))
    route = [(i - distance, i) for i in devices if i - distance in devices]
    return lax.ppermute(block, axis, route)


def prefix(part, axis, combine, identity, reverse):
    count = lax.axis_size(axis)
    place = lax.axis_index(axis)
    ahead = count - 1 - place if reverse else place
    gathered = jax.tree.map(lambda a: lax.all_gather(a, axis), part)
    state = jax.tree.map(lambda a, e: jnp.zeros_like(a) + jnp.asarray(e, a.dtype), part, identity)

    def one(turn, state):
        source = count - 1 - turn if reverse else turn
        return combine(
            state, jax.tree.map(lambda a: lax.dynamic_index_in_dim(a, source, 0, False), gathered)
        )

    return lax.fori_loop(0, ahead, one, state)


def link(first, second):
    return (first[0] * second[0], second[0] * first[1] + second[1])


def per_device(rows_in, cotangent, taps, residues, rates, skip, state_before, adjoint_after):
    batch = rows_in.shape[0]
    seg = rows_in.shape[1]
    chans = rows_in.shape[2] // 3
    width = BLOCK
    blocks = seg // width
    taps_all, res_all, rate_all, skip_row = (
        lax.all_gather(taps, "fsdp", axis=1, tiled=True),
        lax.all_gather(residues, "fsdp", axis=1, tiled=True),
        lax.all_gather(rates, "fsdp", axis=1, tiled=True),
        lax.all_gather(skip[None, :], "fsdp", axis=1, tiled=True),
    )
    skip_all = skip_row[0]
    before = from_behind(rows_in[:, seg - 2 :, :], "ctx", 1)
    extended = jnp.concatenate([before, rows_in], axis=1)
    feat = (
        taps_all[0] * extended[:, 2:]
        + taps_all[1] * extended[:, 1 : seg + 1]
        + taps_all[2] * extended[:, :seg]
    )
    query = feat[..., :chans]
    keys = feat[..., chans : 2 * chans]
    values = feat[..., 2 * chans :]
    mixed = keys * values
    grad_filtered = cotangent * query
    decay = jnp.exp(-rate_all)
    inner = jnp.arange(width, dtype=jnp.float32)
    powers = jnp.exp(-rate_all[None] * inner[:, None, None])
    reverse_powers = powers[::-1]
    lag_weight = inner[:, None, None] * jnp.exp(-rate_all[None] * (inner - 1.0)[:, None, None])
    kernel = jnp.sum(res_all[None] * powers, axis=1)
    mixed_blocks = mixed.reshape(batch, blocks, width, chans)
    grad_blocks = grad_filtered.reshape(batch, blocks, width, chans)
    zeros_pad = jnp.zeros((batch, blocks, width - 1, chans), jnp.float32)
    mixed_pad = jnp.concatenate([zeros_pad, mixed_blocks], axis=2)
    grad_pad = jnp.concatenate([grad_blocks, zeros_pad], axis=2)
    ends_block = jnp.sum(mixed_blocks[:, :, :, None, :] * reverse_powers[None, None], axis=2)
    ends_count = jnp.sum(
        mixed_blocks[:, :, :, None, :]
        * (reverse_powers * (width - 1.0 - inner)[:, None, None])[None, None],
        axis=2,
    )
    starts_block = jnp.sum(grad_blocks[:, :, :, None, :] * powers[None, None], axis=2)
    starts_count = jnp.sum(
        grad_blocks[:, :, :, None, :] * (powers * (inner + 1.0)[:, None, None])[None, None], axis=2
    )
    block_decay = jnp.broadcast_to(jnp.exp(-rate_all * width)[None, None], ends_block.shape)
    inclusive = lax.associative_scan(link, (block_decay, ends_block), axis=1)[1]
    rev_inclusive = lax.associative_scan(link, (block_decay, starts_block), reverse=True, axis=1)[1]
    end_all = inclusive[:, blocks - 1]
    start_all = rev_inclusive[:, 0]
    me = lax.axis_index("ctx")
    is_first = me == 0
    is_last = me == lax.axis_size("ctx") - 1
    span_one = jnp.exp(-rate_all * seg)[None]
    end_all = end_all + jnp.where(is_first, span_one * state_before, 0.0)
    start_all = start_all + jnp.where(is_last, span_one * adjoint_after, 0.0)
    unit = (jnp.ones_like(end_all), jnp.zeros_like(end_all))
    prior = prefix((span_one, end_all), "ctx", link, unit, False)[1]
    after = prefix((span_one, start_all), "ctx", link, unit, True)[1]
    prior = prior + jnp.where(is_first, state_before, 0.0)
    after = after + jnp.where(is_last, adjoint_after, 0.0)
    block_index = jnp.arange(blocks, dtype=jnp.float32) * width
    block_powers = jnp.exp(-rate_all[None] * block_index[:, None, None])
    empty_block = jnp.zeros_like(inclusive[:, :1])
    entry = block_powers[None] * prior[:, None] + jnp.concatenate(
        [empty_block, inclusive[:, : blocks - 1]], axis=1
    )
    leaving = block_powers[::-1][None] * after[:, None] + jnp.concatenate(
        [rev_inclusive[:, 1:], empty_block], axis=1
    )
    carry_weight = res_all[None] * powers * decay[None]
    leave_weight = res_all[None] * reverse_powers * decay[None]
    modal_blocks = jnp.sum(carry_weight[None, None] * entry[:, :, None], axis=3)
    adjoint_blocks = jnp.sum(leave_weight[None, None] * leaving[:, :, None], axis=3)
    lag_terms = []
    for lag in range(width):
        mixed_lag = mixed_pad[:, :, width - 1 - lag : 2 * width - 1 - lag]
        modal_blocks = modal_blocks + kernel[lag] * mixed_lag
        adjoint_blocks = adjoint_blocks + kernel[lag] * grad_pad[:, :, lag : lag + width]
        lag_terms.append(jnp.sum(grad_blocks * mixed_lag, axis=(0, 1, 2)))
    correlation = jnp.stack(lag_terms)
    modal = modal_blocks.reshape(batch, seg, chans)
    adjoint = adjoint_blocks.reshape(batch, seg, chans)
    res_sum = decay * jnp.sum(entry * starts_block, axis=(0, 1)) + jnp.sum(
        powers * correlation[:, None, :], axis=0
    )
    rate_sum = width * jnp.exp(-rate_all * width) * jnp.sum(entry * leaving, axis=(0, 1))
    rate_sum = (
        rate_sum
        + jnp.sum(entry * starts_count, axis=(0, 1))
        + jnp.sum(leaving * ends_count, axis=(0, 1))
    )
    rate_sum = rate_sum + jnp.sum(lag_weight * correlation[:, None, :], axis=0)
    filtered = modal + skip_all * mixed
    grad_query = cotangent * filtered
    grad_mixed = adjoint + skip_all * grad_filtered
    grad_feat = jnp.concatenate([grad_query, grad_mixed * values, grad_mixed * keys], axis=2)
    following = from_behind(grad_feat[:, :2], "ctx", -1)
    padded = jnp.concatenate([grad_feat, following], axis=1)
    grad_rows = (
        taps_all[0] * grad_feat
        + taps_all[1] * padded[:, 1 : seg + 1]
        + taps_all[2] * padded[:, 2 : seg + 2]
    ).astype(jnp.bfloat16)
    scale = lax.rsqrt(jnp.float32(batch * seg * lax.axis_size("ctx") * lax.axis_size("fsdp")))
    tap_terms = (
        jnp.stack(
            [
                jnp.sum(extended[:, 2 - shift_by : 2 - shift_by + seg] * grad_feat, axis=(0, 1))
                for shift_by in range(3)
            ]
        )
        * scale
    )
    res_terms = res_sum * scale
    rate_terms = -decay * res_all * rate_sum * scale
    skip_terms = jnp.sum(grad_filtered * mixed, axis=(0, 1))[None, :] * scale
    shares = (
        lax.psum_scatter(tap_terms, "fsdp", scatter_dimension=1, tiled=True),
        lax.psum_scatter(res_terms, "fsdp", scatter_dimension=1, tiled=True),
        lax.psum_scatter(rate_terms, "fsdp", scatter_dimension=1, tiled=True),
        lax.psum_scatter(skip_terms, "fsdp", scatter_dimension=1, tiled=True),
    )
    totals = lax.psum((shares[0], shares[1], shares[2], shares[3]), "ctx")
    return (grad_rows, totals[0], totals[1], totals[2], totals[3][0])


def solution(mesh):
    in_specs = (
        P("fsdp", "ctx", None),
        P("fsdp", "ctx", None),
        P(None, "fsdp"),
        P(None, "fsdp"),
        P(None, "fsdp"),
        P("fsdp"),
        P("fsdp", None, None),
        P("fsdp", None, None),
    )
    out_specs = (
        P("fsdp", "ctx", None),
        P(None, "fsdp"),
        P(None, "fsdp"),
        P(None, "fsdp"),
        P("fsdp"),
    )
    return jax.shard_map(
        per_device, mesh=mesh, in_specs=in_specs, out_specs=out_specs, check_vma=False
    )
```

profile of v0, /device:TPU:1, one launch (start us, length us, event | category | flops | bytes accessed | tf_op | source)
XLA Modules:
  0.0 958.7 jit_solution(10816614960031255710)
XLA Ops:
  9.0 10.2 %collective-permute-start = (bf16[1,2,12288]{2,1,0:T(2,128)(2,1)S(1)}, bf16[1,2,12288]{2,1,0:T(2,128)(2,1)S(1)}, u32[]{:S(2)}, u32[]{:S(2)}) collective-permute-start(bf16[1,2,12288]{2,1,0:T(2,128)(2,1)S(1)} %slice.346), channel_id=1, source_target_pairs={{0,16},{16,32},{32,48},{48,64},{64,80},{80,96},{96,112},{112,128},... | collective-permute-start | bytes 147464 | tf_op jit(solution)/shard_map/ppermute | solution.py:12
  19.3 36.4 %all_gather.30 = f32[16,4096]{1,0:T(8,128)S(1)} all-gather(f32[16,256]{1,0:T(8,128)} %param.16), channel_id=1, replica_groups=mesh['ctx'=16,'fsdp'=16] {'fsdp'}, dimensions={1}, use_global_device_ids=true | all-gather | bytes 278528 | tf_op jit(solution)/shard_map/all_gather | solution.py:44
  57.8 33.5 %all_gather.28 = f32[3,12288]{1,0:T(4,128)S(1)} all-gather(f32[3,768]{1,0:T(4,128)S(1)} %copy-done.56), channel_id=1, replica_groups=mesh['ctx'=16,'fsdp'=16] {'fsdp'}, dimensions={1}, use_global_device_ids=true | all-gather | bytes 156672 | tf_op jit(solution)/shard_map/all_gather | solution.py:42
  93.9 40.0 %all_gather.29 = f32[16,4096]{1,0:T(8,128)S(1)} all-gather(f32[16,256]{1,0:T(8,128)S(1)} %copy-done.55), channel_id=1, replica_groups=mesh['ctx'=16,'fsdp'=16] {'fsdp'}, dimensions={1}, use_global_device_ids=true | all-gather | bytes 278528 | tf_op jit(solution)/shard_map/all_gather | solution.py:43
  134.5 4.7 rev.4
  139.2 5.6 fusion.1
  147.4 4.6 multiply_reduce_fusion.9
  154.1 8.5 broadcast_multiply_fusion
  162.7 14.8 %multiply_reduce_fusion = (f32[8,16,4096]{2,1,0:T(8,128)}, f32[8,16,4096]{2,1,0:T(8,128)S(1)}, f32[8,16,4096]{2,1,0:T(8,128)}, f32[8,16,4096]{2,1,0:T(8,128)}) fusion(f32[16,16,4096]{2,1,0:T(8,128)S(1)} %get-tuple-element.225, f32[8,16,4096]{2,1,0:T(8,128)S(1)} %bitcast.177, f32[16,16,4096]{2,1,0:T(8,128)} %rev.4, f32[16,16,4096]{2,1,0:T(8,128)S(1)} %copy-done, ...), kind=kLoop, calls=%fused_computation.4 | loop fusion | flops 65011712 | bytes 29360128 | tf_op jit(solution)/shard_map/reduce_sum | solution.py:72
  214.4 4.7 pad.172
  223.0 4.7 pad.52
  233.4 35.1 %all-gather.4 = f32[16,1,256]{2,1,0:T(1,128)} all-gather(f32[1,1,256]{2,1,0:T(1,128)} %bitcast.255), channel_id=4, replica_groups=mesh['ctx'=16,'fsdp'=16] {'fsdp'}, dimensions={0}, use_global_device_ids=true | all-gather | bytes 17408 | tf_op jit(solution)/shard_map/all_gather | solution.py:45
  271.2 4.6 pad.80
  275.8 3.5 slice_add_fusion.6
  283.1 3.5 slice_add_fusion.5
  286.5 34.7 %all-gather.11.cloned.1.call-done = f32[16,16,4096]{2,1,0:T(8,128)} async-done(((f32[1,16,4096]{2,1,0:T(8,128)}), f32[16,16,4096]{2,1,0:T(8,128)}) %all-gather.11.cloned.1.call-update) | async-done | bytes 4194320 | tf_op jit(solution)/shard_map/all_gather | solution.py:19
  322.5 74.2 %all-gather.13.cloned.1.call-done = f32[16,16,4096]{2,1,0:T(8,128)} async-done(((f32[1,16,4096]{2,1,0:T(8,128)}), f32[16,16,4096]{2,1,0:T(8,128)}) %all-gather.13.cloned.1.call-update) | async-done | bytes 4194320 | tf_op jit(solution)/shard_map/all_gather | solution.py:19
  396.8 16.7 %while.27 = (s32[]{:T(128)}, f32[1,16,4096]{2,1,0:T(8,128)S(1)}, s32[]{:T(128)}, f32[16,1,16,4096]{3,2,1,0:T(8,128)}, f32[16,1,16,4096]{3,2,1,0:T(8,128)}, /*index=5*/s32[]{:T(128)}, s32[]{:T(128)}, s32[]{:T(128)}, s32[]{:T(128)}) while((s32[]{:T(128)}, f32[1,16,4096]{2,1,0:T(8,128)S(1)}, s32[]{:T(128)}, f32[16,1,16,4096]{3,2,1,0:T(8,128)}, ...), condition=%wide.region_7.8_spmd, body=%wide.region_6.7_spmd.sunk | while | flops 131078 | bytes 1048719 | solution.py:28
  413.5 7.3 multiply_reduce_fusion.8
  420.9 9.6 %multiply_reduce_fusion.4 = f32[8,16,4096]{2,1,0:T(8,128)} fusion(f32[8,16,4096]{2,1,0:T(8,128)S(1)} %get-tuple-element.227, f32[16,16,4096]{2,1,0:T(8,128)S(1)} %copy-done.11), kind=kLoop, calls=%fused_computation.8 | loop fusion | flops 16252928 | bytes 8388608 | tf_op jit(solution)/shard_map/reduce_sum | solution.py:108
  430.6 9.6 %multiply_reduce_fusion.2 = f32[8,16,4096]{2,1,0:T(8,128)} fusion(f32[8,16,4096]{2,1,0:T(8,128)S(1)} %get-tuple-element.224, f32[16,16,4096]{2,1,0:T(8,128)S(1)} %copy-done.10), kind=kLoop, calls=%fused_computation.6 | loop fusion | flops 16252928 | bytes 8388608 | tf_op jit(solution)/shard_map/reduce_sum | solution.py:109
  440.4 5.7 fusion.59
  446.0 14.4 %fusion.28 = f32[1,8,16,4096]{3,2,1,0:T(8,128)S(1)} fusion(f32[1,8,16,4096]{3,2,1,0:T(8,128)} %bitcast.180, f32[8,16,4096]{2,1,0:T(8,128)} %multiply_reduce_fusion.2, f32[4096]{0:T(1024)S(1)} %bitcast.206, f32[4096]{0:T(1024)S(1)} %bitcast.208, f32[4096]{0:T(1024)S(1)} %bitcast.210, f32[4096]{0:T(1024)S(1)} %bitcast.212, f32[4096]{0:T(1024)S(1)} %bitcast.214, ...), kind=kLoop, calls=%fused_computation.87 | loop fusion | flops 16777216 | bytes 6553600 | tf_op jit(solution)/shard_map/add | solution.py:114
  469.5 3.6 collective-permute-start.1
  475.2 4.1 collective-permute-done.1
  482.1 10.6 %fusion.3 = (f32[12288]{0:T(1024)S(1)}, f32[12288]{0:T(1024)S(1)}, f32[12288]{0:T(1024)S(1)}, bf16[1,128,12288]{2,1,0:T(8,128)(2,1)}) fusion(bf16[1,128,12288]{2,1,0:T(8,128)(2,1)} %param.12, bf16[1,2,12288]{2,1,0:T(2,128)(2,1)S(1)} %copy-done.37, f32[1,128,4096]{2,1,0:T(8,128)} %copy-done.7, f32[1,128,4096]{2,1,0:T(8,128)S(1)} %copy-done.6, ...), kind=kLoop, calls=%fused_computation.50 | loop fusion | flops 36139008 | bytes 25509888 | tf_op jit(solution)/shard_map/reduce_sum | solution.py:144
  492.9 4.0 copy.25
  500.1 52.6 %reduce-scatter.15.cloned.1.call-done = f32[256,1]{1,0:T(8,128)} async-done(((f32[4096,1]{1,0:T(8,128)}), f32[256,1]{1,0:T(8,128)}) %reduce-scatter.15.cloned.1.call-update) | async-done | bytes 1040
  553.7 152.7 %reduce-scatter.13.cloned.1.call-done = f32[768,3]{1,0:T(8,128)} async-done(((f32[12288,3]{1,0:T(8,128)}), f32[768,3]{1,0:T(8,128)}) %reduce-scatter.13.cloned.1.call-update) | async-done | bytes 9232
  707.6 71.1 %reduce-scatter.11.cloned.1.call-done = f32[16,256]{1,0:T(8,128)} async-done(((f32[16,4096]{1,0:T(8,128)}), f32[16,256]{1,0:T(8,128)}) %reduce-scatter.11.cloned.1.call-update) | async-done | bytes 16400 | tf_op jit(solution)/shard_map/reduce_scatter | solution.py:156
  778.7 82.6 %reduce-scatter.9.cloned.1.call-done = f32[16,256]{1,0:T(8,128)} async-done(((f32[16,4096]{1,0:T(8,128)}), f32[16,256]{1,0:T(8,128)}) %reduce-scatter.9.cloned.1.call-update) | async-done | bytes 16400 | tf_op jit(solution)/shard_map/reduce_scatter | solution.py:155
  861.2 90.1 %all-reduce.16 = (f32[3,768]{1,0:T(4,128)}, f32[16,256]{1,0:T(8,128)}, f32[16,256]{1,0:T(8,128)}, f32[256]{0:T(256)}) all-reduce(f32[3,768]{1,0:T(4,128)S(1)} %copy.26, f32[16,256]{1,0:T(8,128)} %reduce-scatter.9.cloned.1.call-done, f32[16,256]{1,0:T(8,128)} %reduce-scatter.11.cloned.1.call-done, ...), channel_id=1, replica_groups=mesh['ctx'=16,'fsdp'=16] {'ctx'}, use_global_device_ids=true, to_apply=%region_13.14 | all-reduce | flops 10752 | bytes 86016 | tf_op jit(solution)/shard_map/psum | solution.py:159
  (205 shorter events, 102.3 us)
Async XLA Ops:
  8.0 49.8 %copy-start.56 = (f32[3,768]{1,0:T(4,128)S(1)}, f32[3,768]{1,0:T(4,128)}, u32[]{:S(2)}) copy-start(f32[3,768]{1,0:T(4,128)} %param.14) | copy-start | bytes 27652
  8.0 278.5 %all-gather.9.cloned.1.call-start = ((), (), s32[]{:S(2)}) async-start(), calls=%async_computation.6 | async-start | bytes 4456448 | tf_op jit(solution)/shard_map/all_gather | solution.py:19
  9.0 130.1 %collective-permute-start = (bf16[1,2,12288]{2,1,0:T(2,128)(2,1)S(1)}, bf16[1,2,12288]{2,1,0:T(2,128)(2,1)S(1)}, u32[]{:S(2)}, u32[]{:S(2)}) collective-permute-start(bf16[1,2,12288]{2,1,0:T(2,128)(2,1)S(1)} %slice.346), channel_id=1, source_target_pairs={{0,16},{16,32},{32,48},{48,64},{64,80},{80,96},{96,112},{112,128},... | collective-permute-start | bytes 147464 | tf_op jit(solution)/shard_map/ppermute | solution.py:12
  56.6 97.5 %copy-start.15 = (f32[16,4096]{1,0:T(8,128)}, f32[16,4096]{1,0:T(8,128)S(1)}, u32[]{:S(2)}) copy-start(f32[16,4096]{1,0:T(8,128)S(1)} %get-tuple-element.256) | copy-start | bytes 786436
  56.6 264.6 %all-gather.11.cloned.1.call-start = ((), (), s32[]{:S(2)}) async-start(), calls=%async_computation.7 | async-start | bytes 4456448 | tf_op jit(solution)/shard_map/all_gather | solution.py:19
  133.9 20.2 %copy-start.21 = (f32[16,4096]{1,0:T(8,128)}, f32[16,4096]{1,0:T(8,128)S(1)}, u32[]{:S(2)}) copy-start(f32[16,4096]{1,0:T(8,128)S(1)} %all_gather.29) | copy-start | bytes 786436
  229.9 166.8 %all-gather.13.cloned.1.call-start = ((), (), s32[]{:S(2)}) async-start(), calls=%async_computation.8 | async-start | bytes 4456448 | tf_op jit(solution)/shard_map/all_gather | solution.py:19
  230.7 322.1 %reduce-scatter.15.cloned.1.call-start = ((), (), s32[]{:S(2)}) async-start(), calls=%async_computation.10 | async-start | bytes 2228224
  396.7 16.7 %copy-start.29 = (f32[1,16,4096]{2,1,0:T(8,128)S(1)}, f32[1,16,4096]{2,1,0:T(8,128)}, u32[]{:S(2)}) copy-start(f32[1,16,4096]{2,1,0:T(8,128)} %param.19) | copy-start | bytes 786436
  396.7 16.8 %copy-start.16 = (f32[16,4096]{1,0:T(8,128)S(1)}, f32[16,4096]{1,0:T(8,128)}, u32[]{:S(2)}) copy-start(f32[16,4096]{1,0:T(8,128)} %copy-done.15) | copy-start | bytes 786436
  430.5 9.7 %copy-start.38 = (f32[1,4096]{1,0:T(1,128)S(1)}, f32[1,4096]{1,0:T(1,128)}, u32[]{:S(2)}) copy-start(f32[1,4096]{1,0:T(1,128)} %get-tuple-element.257) | copy-start | bytes 49156
  430.5 9.7 %copy-start.39 = (f32[1,4096]{1,0:T(1,128)S(1)}, f32[1,4096]{1,0:T(1,128)}, u32[]{:S(2)}) copy-start(f32[1,4096]{1,0:T(1,128)} %get-tuple-element.258) | copy-start | bytes 49156
  430.5 9.7 %copy-start.40 = (f32[1,4096]{1,0:T(1,128)S(1)}, f32[1,4096]{1,0:T(1,128)}, u32[]{:S(2)}) copy-start(f32[1,4096]{1,0:T(1,128)} %get-tuple-element.259) | copy-start | bytes 49156
  430.5 9.7 %copy-start.41 = (f32[1,4096]{1,0:T(1,128)S(1)}, f32[1,4096]{1,0:T(1,128)}, u32[]{:S(2)}) copy-start(f32[1,4096]{1,0:T(1,128)} %get-tuple-element.260) | copy-start | bytes 49156
  430.5 9.7 %copy-start.42 = (f32[1,4096]{1,0:T(1,128)S(1)}, f32[1,4096]{1,0:T(1,128)}, u32[]{:S(2)}) copy-start(f32[1,4096]{1,0:T(1,128)} %get-tuple-element.261) | copy-start | bytes 49156
  430.5 9.7 %copy-start.43 = (f32[1,4096]{1,0:T(1,128)S(1)}, f32[1,4096]{1,0:T(1,128)}, u32[]{:S(2)}) copy-start(f32[1,4096]{1,0:T(1,128)} %get-tuple-element.262) | copy-start | bytes 49156
  430.5 9.7 %copy-start.44 = (f32[1,4096]{1,0:T(1,128)S(1)}, f32[1,4096]{1,0:T(1,128)}, u32[]{:S(2)}) copy-start(f32[1,4096]{1,0:T(1,128)} %get-tuple-element.263) | copy-start | bytes 49156
  430.5 9.7 %copy-start.45 = (f32[1,4096]{1,0:T(1,128)S(1)}, f32[1,4096]{1,0:T(1,128)}, u32[]{:S(2)}) copy-start(f32[1,4096]{1,0:T(1,128)} %get-tuple-element.264) | copy-start | bytes 49156
  430.6 9.7 %copy-start.46 = (f32[1,4096]{1,0:T(1,128)S(1)}, f32[1,4096]{1,0:T(1,128)}, u32[]{:S(2)}) copy-start(f32[1,4096]{1,0:T(1,128)} %get-tuple-element.265) | copy-start | bytes 49156
  430.6 9.7 %copy-start.47 = (f32[1,4096]{1,0:T(1,128)S(1)}, f32[1,4096]{1,0:T(1,128)}, u32[]{:S(2)}) copy-start(f32[1,4096]{1,0:T(1,128)} %get-tuple-element.266) | copy-start | bytes 49156
  430.6 9.7 %copy-start.48 = (f32[1,4096]{1,0:T(1,128)S(1)}, f32[1,4096]{1,0:T(1,128)}, u32[]{:S(2)}) copy-start(f32[1,4096]{1,0:T(1,128)} %get-tuple-element.267) | copy-start | bytes 49156
  430.6 9.7 %copy-start.49 = (f32[1,4096]{1,0:T(1,128)S(1)}, f32[1,4096]{1,0:T(1,128)}, u32[]{:S(2)}) copy-start(f32[1,4096]{1,0:T(1,128)} %get-tuple-element.268) | copy-start | bytes 49156
  430.6 9.7 %copy-start.50 = (f32[1,4096]{1,0:T(1,128)S(1)}, f32[1,4096]{1,0:T(1,128)}, u32[]{:S(2)}) copy-start(f32[1,4096]{1,0:T(1,128)} %get-tuple-element.269) | copy-start | bytes 49156
  430.6 9.7 %copy-start.51 = (f32[1,4096]{1,0:T(1,128)S(1)}, f32[1,4096]{1,0:T(1,128)}, u32[]{:S(2)}) copy-start(f32[1,4096]{1,0:T(1,128)} %get-tuple-element.270) | copy-start | bytes 49156
  430.6 9.7 %copy-start.52 = (f32[1,4096]{1,0:T(1,128)S(1)}, f32[1,4096]{1,0:T(1,128)}, u32[]{:S(2)}) copy-start(f32[1,4096]{1,0:T(1,128)} %get-tuple-element.271) | copy-start | bytes 49156
  446.0 14.4 %copy-start.3 = (f32[1,128,4096]{2,1,0:T(8,128)S(1)}, f32[1,128,4096]{2,1,0:T(8,128)}, u32[]{:S(2)}) copy-start(f32[1,128,4096]{2,1,0:T(8,128)} %copy-done.1) | copy-start | bytes 6291460
  446.0 14.4 %copy-start.13 = (f32[1,8,16,4096]{3,2,1,0:T(8,128)S(1)}, f32[1,8,16,4096]{3,2,1,0:T(8,128)}, u32[]{:S(2)}) copy-start(f32[1,8,16,4096]{3,2,1,0:T(8,128)} %fusion.59) | copy-start | bytes 6291460
  446.0 14.4 %copy-start.20 = (bf16[1,128,4096]{2,1,0:T(8,128)(2,1)S(1)}, bf16[1,128,4096]{2,1,0:T(8,128)(2,1)}, u32[]{:S(2)}) copy-start(bf16[1,128,4096]{2,1,0:T(8,128)(2,1)} %param.13) | copy-start | bytes 3145732
  469.5 9.8 %collective-permute-start.1 = (f32[1,2,12288]{2,1,0:T(2,128)S(1)}, f32[1,2,12288]{2,1,0:T(2,128)S(1)}, u32[]{:S(2)}, u32[]{:S(2)}) collective-permute-start(f32[1,2,12288]{2,1,0:T(2,128)S(1)} %slice.494), channel_id=1, source_target_pairs={{16,0},{32,16},{48,32},{64,48},{80,64},{96,80},{112,96},{128,112},... | collective-permute-start | bytes 294920 | tf_op jit(solution)/shard_map/ppermute | solution.py:12
  475.2 231.2 %reduce-scatter.13.cloned.1.call-start = ((), (), s32[]{:S(2)}) async-start(), calls=%async_computation.9 | async-start | bytes 6684672
  497.0 281.7 %reduce-scatter.11.cloned.1.call-start = ((), (), s32[]{:S(2)}) async-start(), calls=%async_computation.5 | async-start | bytes 278528 | tf_op jit(solution)/shard_map/reduce_scatter | solution.py:156
  499.4 361.8 %reduce-scatter.9.cloned.1.call-start = ((), (), s32[]{:S(2)}) async-start(), calls=%async_computation.4 | async-start | bytes 278528 | tf_op jit(solution)/shard_map/reduce_scatter | solution.py:155
  (34 other events, 128.5 us)
Sparse Core Ops, SparseCore 0:
  56.7 79.6 all-gather.8
  230.1 91.1 all-gather.10
  323.9 72.7 all-gather.12
Sparse Core Ops, SparseCore 1:
  475.2 77.4 reduce-scatter.14
  555.2 151.2 reduce-scatter.12
  708.8 69.8 reduce-scatter.10
  781.3 79.8 reduce-scatter.8
where the time goes:
time: 965 us; the launch traced here: 959 us
  waiting for transfers between devices  473 us (49%)
  blocking collectives  235 us (24%)
  other arithmetic  157 us (16%)
  local copies, waits for them, and re-layouts  63 us (7%)
  between operations  16.2 us (2%)
  starting transfers between devices  14.1 us (1%)
    unnamed x9, waiting for transfers between devices  206 us
    all_gather x3, waiting for transfers between devices, prefix(): gathered = jax.tree.map(lambda a: lax.all_gather(a, axis), part)  109 us
    psum x1, blocking collectives, per_device(): totals = lax.psum((shares[0], shares[1], shares[2], shares[3]), 'ctx')  90.1 us
    reduce_scatter x1, waiting for transfers between devices, per_device(): lax.psum_scatter(res_terms, 'fsdp', scatter_dimension=1, tiled=True)  82.6 us
    reduce_scatter x1, waiting for transfers between devices, per_device(): lax.psum_scatter(rate_terms, 'fsdp', scatter_dimension=1, tiled=True)  71.1 us
    all_gather x1, blocking collectives, per_device(): lax.all_gather(residues, 'fsdp', axis=1, tiled=True)  40 us
    all_gather x1, blocking collectives, per_device(): lax.all_gather(rates, 'fsdp', axis=1, tiled=True)  36.4 us
    all_gather x1, blocking collectives, per_device(): lax.all_gather(skip[None, :], 'fsdp', axis=1, tiled=True)  35.1 us
  transfers between devices with their start and end apart: 9, of which 7 were waited for; matrix products, arithmetic and copies ran while one was open for 15% of the time, Pallas kernels for 0%

commit v1 on v0

v1 whole, which is shorter than its diff:
```python
import math

import jax
import jax.numpy as jnp
from jax import lax
from jax.experimental import pallas as pl
from jax.experimental.pallas import tpu as pltpu
from jax.sharding import PartitionSpec as P

MESH = pl.DeviceIdType.MESH
F32 = jnp.float32
MODES = 16
LANES = 128
STEPS = 16
OWNERS = 16
ROWS = 96
HALF = ROWS // 2
PARTS = 4
PIECE = OWNERS // PARTS
GROUPS = 4
GRID = 32 // GROUPS
VMEM = pl.BlockSpec(memory_space=pltpu.VMEM)


def place():
    p = lax.axis_index("ctx")
    f = lax.axis_index("fsdp")
    return p, f, p % 2, (p // 2) % 2, p // 4


def remote(src, dst, send, recv, ctx, fsdp):
    return pltpu.make_async_remote_copy(
        src_ref=src, dst_ref=dst, send_sem=send, recv_sem=recv,
        device_id=(ctx, fsdp), device_id_type=MESH,
    )


def greet(ctx, fsdp):
    pl.semaphore_signal(
        pltpu.get_barrier_semaphore(), inc=1, device_id=(ctx, fsdp), device_id_type=MESH
    )


def gather_kernel(res, rate, taps, skip, tail, head, gath, prev, nxt, pbuf, nbuf,
                  send, recv, csend, crecv, hsend, hrecv):
    p, f, c, _, _ = place()
    partner = p + 1 - 2 * c
    for step in range(1, OWNERS):
        greet(p, (f + step) % OWNERS)
    outer = (p + 15 + 2 * c) % 16
    greet(partner, f)
    greet(outer, f)

    mine = gath.at[f]
    for b in range(2):
        cols = slice(LANES * b, LANES * (b + 1))
        gath[f, 16 * b : 16 * (b + 1), :] = res[:, cols]
        gath[f, 32 + 16 * b : 48 + 16 * b, :] = rate[:, cols]
        gath[f, 82 + b : 83 + b, :] = skip[:, cols]
    for j in range(3):
        for b in range(6):
            row = 64 + 6 * j + b
            gath[f, row : row + 1, :] = taps[j : j + 1, LANES * b : LANES * (b + 1)]
    gath[f, 84:96, :] = jnp.zeros((12, LANES), F32)
    pl.semaphore_wait(pltpu.get_barrier_semaphore(), OWNERS + 1)

    first = pl.multiple_of(c * HALF, 8)
    own = mine.at[pl.ds(first, HALF)]
    out = []
    for step in range(1, OWNERS):
        to = (f + step) % OWNERS
        copy = remote(own, own, send.at[step], recv.at[step], p, to)
        copy.start()
        out.append(copy)
    right = remote(tail, pbuf, hsend.at[0], hrecv.at[0], p + 1, f)
    left = remote(head, nbuf, hsend.at[1], hrecv.at[1], p - 1, f)

    @pl.when(p < 15)
    def _():
        right.start()

    @pl.when(p > 0)
    def _():
        left.start()

    for step in range(1, OWNERS):
        source = (f + OWNERS - step) % OWNERS
        block = gath.at[source, pl.ds(first, HALF)]
        remote(block, block, send.at[step], recv.at[step], p, f).wait_recv()
        copy = remote(block, block, csend.at[step], crecv.at[step], partner, f)
        copy.start()
        out.append(copy)

    @pl.when(p > 0)
    def _():
        right.wait_recv()
        prev[...] = pbuf[...].astype(F32)

    @pl.when(p == 0)
    def _():
        prev[...] = jnp.zeros_like(prev)

    @pl.when(p < 15)
    def _():
        left.wait_recv()
        nxt[...] = nbuf[...].astype(F32)

    @pl.when(p == 15)
    def _():
        nxt[...] = jnp.zeros_like(nxt)

    other = pl.multiple_of(HALF - c * HALF, 8)
    for step in range(1, OWNERS):
        source = (f + OWNERS - step) % OWNERS
        block = gath.at[source, pl.ds(other, HALF)]
        remote(block, block, csend.at[step], crecv.at[step], partner, f).wait_recv()
    for copy in out:
        copy.wait_send()

    @pl.when(p < 15)
    def _():
        right.wait_send()

    @pl.when(p > 0)
    def _():
        left.wait_send()


def spread(row):
    return jnp.broadcast_to(row, (8, LANES))


def sublane():
    return lax.broadcasted_iota(jnp.int32, (8, LANES), 0)


def tap_place(section, group, j):
    unit = section * 32 + group
    return unit // 6, pl.ds(64 + 6 * j + unit % 6, 1)


def own_rows(group, first, count):
    base = (group % 2) * MODES
    if count == MODES:
        base = pl.multiple_of(base, MODES)
    return group // 2, pl.ds(base + first, count)


def skip_place(group):
    return group // 2, pl.ds(82 + group % 2, 1)


def features(refs, cot_ref, gath, prev, xs, lanes, group):
    top = sublane() == 0
    raw, lag1, lag2, feat = [], [], [], []
    for q in range(3):
        xs[q, :, :] = refs[q][0, :, lanes].astype(F32)
        x = [xs[q, pl.ds(i, 8, stride=STEPS), :] for i in range(STEPS)]
        far = prev[pl.ds(q * 32 + group, 1), :]
        near = prev[pl.ds(96 + q * 32 + group, 1), :]
        before1 = jnp.where(top, spread(near), pltpu.roll(x[15], 1, 0))
        before2 = jnp.where(top, spread(far), pltpu.roll(x[14], 1, 0))
        one = [before1] + x[:15]
        two = [before2, before1] + x[:14]
        t = [spread(gath[tap_place(q, group, j)]) for j in range(3)]
        raw.append(x)
        lag1.append(one)
        lag2.append(two)
        feat.append([t[0] * x[i] + t[1] * one[i] + t[2] * two[i] for i in range(STEPS)])
    xs[3, :, :] = cot_ref[0, :, lanes].astype(F32)
    cot = [xs[3, pl.ds(i, 8, stride=STEPS), :] for i in range(STEPS)]
    return raw, lag1, lag2, feat, cot


def local_kernel(q_ref, k_ref, v_ref, cot_ref, gath, prev, ends, starts, e_out, s_out,
                 xs, us, gs, weights):
    block = pl.program_id(0)
    sub = sublane()

    def one(j, _):
        group = block * GROUPS + j
        lanes = pl.ds(pl.multiple_of(j * LANES, LANES), LANES)
        _, _, _, feat, cot = features((q_ref, k_ref, v_ref), cot_ref, gath, prev, xs, lanes, group)
        for i in range(STEPS):
            us[i] = feat[1][i] * feat[2][i]
            gs[i] = cot[i] * feat[0][i]
        rate = gath[own_rows(group, 32, MODES)]
        weights[0] = jnp.exp(-rate)
        weights[1] = jnp.exp(-16.0 * rate)
        weights[2] = jnp.exp(-32.0 * rate)
        weights[3] = jnp.exp(-64.0 * rate)
        for base in range(0, MODES, 8):
            modes = range(base, base + 8)
            d = [spread(weights[0, m : m + 1, :]) for m in modes]
            e = [us[0]] * 8
            b = [gs[15]] * 8
            for i in range(1, STEPS):
                u, g = us[i], gs[15 - i]
                e = [d[n] * e[n] + u for n in range(8)]
                b = [d[n] * b[n] + g for n in range(8)]
            for n, m in enumerate(modes):
                fwd, bwd = e[n], b[n]
                for power, shift in ((1, 1), (2, 2), (3, 4)):
                    w = spread(weights[power, m : m + 1, :])
                    fwd = fwd + jnp.where(sub >= shift, w, 0.0) * pltpu.roll(fwd, shift, 0)
                    bwd = bwd + jnp.where(sub < 8 - shift, w, 0.0) * pltpu.roll(bwd, 8 - shift, 0)
                ends[j, m] = fwd
                starts[j, m] = bwd
                e_out[own_rows(group, m, 1)] = fwd[7:8]
                s_out[own_rows(group, m, 1)] = bwd[0:1]
        return 0

    lax.fori_loop(0, GROUPS, one, 0)


def prefix_kernel(e_in, s_in, gath, before, after, e_prior, s_prior,
                  first, second, third, whole, last, agg, chip, begin, inner,
                  s1, r1, s2, r2, s3, r3, s4, r4, s5, r5):
    p, f, c, h, x = place()
    partner = p + 1 - 2 * c
    across = p + 2 - 4 * h
    n = jnp.where(c == 1, x, 3 - x)
    sign = jnp.where(c == 1, 4, -4)
    resident = h == c
    greet(partner, f)
    greet(across, f)
    for step in range(1, 4):
        greet((x + step) % 4 * 4 + 2 * h + c, f)
    pl.semaphore_wait(pltpu.get_barrier_semaphore(), 5)

    def piece(a):
        return pl.ds(a * PIECE, PIECE)

    def copy1(a, ref):
        return remote(ref.at[piece(a)], first.at[piece(a)], s1.at[a], r1.at[a], partner, f)

    def copy2(a):
        return remote(agg.at[piece(a)], second.at[piece(a)], s2.at[a], r2.at[a], across, f)

    def copy3(a, j):
        return remote(chip.at[piece(a)], third.at[j - 1, piece(a)], s3.at[j - 1, a], r3.at[j - 1, a],
                      p + sign * j, f)

    def copy4(a):
        return remote(begin.at[piece(a)], whole.at[piece(a)], s4.at[a], r4.at[a], across, f)

    def copy5(a, ref):
        return remote(ref.at[piece(a)], last.at[piece(a)], s5.at[a], r5.at[a], partner, f)

    def decay(a, power):
        return jnp.exp(gath[piece(a), 32:64, :] * (-128.0 * power))

    for a in range(PARTS):
        @pl.when(c == 0)
        def _():
            copy1(a, e_in).start()

        @pl.when(c == 1)
        def _():
            copy1(a, s_in).start()

    for a in range(PARTS):
        copy1(a, e_in).wait_recv()
        mine = jnp.where(c == 1, e_in[piece(a)], s_in[piece(a)])
        agg[piece(a)] = mine + decay(a, 1) * first[piece(a)]

        @pl.when(jnp.logical_not(resident))
        def _():
            copy2(a).start()

    for a in range(PARTS):
        @pl.when(resident)
        def _():
            copy2(a).wait_recv()
            chip[piece(a)] = agg[piece(a)] + decay(a, 2) * second[piece(a)]
            for j in range(1, 4):
                @pl.when(n + j < 4)
                def _():
                    copy3(a, j).start()

    for a in range(PARTS):
        @pl.when(resident)
        def _():
            for o in range(PIECE):
                for b in range(2):
                    at = (2 * (a * PIECE + o) + b) * LANES
                    cols = slice(at, at + LANES)
                    begin[a * PIECE + o, 16 * b : 16 * (b + 1), :] = jnp.where(
                        c == 1, before[0, :, cols], after[0, :, cols]
                    )
            span = decay(a, 4)
            for j in range(3, 0, -1):
                @pl.when(n >= j)
                def _():
                    copy3(a, j).wait_recv()
                    begin[piece(a)] = third[j - 1, piece(a)] + span * begin[piece(a)]
            copy4(a).start()
            inner[piece(a)] = decay(a, 2) * begin[piece(a)] + second[piece(a)]
            copy5(a, inner).start()

        @pl.when(jnp.logical_not(resident))
        def _():
            copy4(a).wait_recv()
            copy5(a, whole).start()

        head = jnp.where(resident, inner[piece(a)], whole[piece(a)])
        agg_own = decay(a, 1) * head + first[piece(a)]

        @pl.when(c == 1)
        def _():
            e_prior[piece(a)] = agg_own

        @pl.when(c == 0)
        def _():
            s_prior[piece(a)] = agg_own

    for a in range(PARTS):
        copy5(a, whole).wait_recv()

        @pl.when(c == 1)
        def _():
            s_prior[piece(a)] = last[piece(a)]

        @pl.when(c == 0)
        def _():
            e_prior[piece(a)] = last[piece(a)]

    for a in range(PARTS):
        copy1(a, e_in).wait_send()

        @pl.when(resident)
        def _():
            for j in range(1, 4):
                @pl.when(n + j < 4)
                def _():
                    copy3(a, j).wait_send()
            copy4(a).wait_send()

        @pl.when(jnp.logical_not(resident))
        def _():
            copy2(a).wait_send()
        copy5(a, whole).wait_send()


def row_sum(x):
    return jnp.sum(x, axis=0, keepdims=True)


def main_kernel(q_ref, k_ref, v_ref, cot_ref, gath, prev, nxt, ends, starts, e_in, e_prior, s_prior,
                out, grads, xs, us, gs, fs, hist, filt, back, weights):
    block = pl.program_id(0)
    sub = sublane()
    edge = lax.axis_index("ctx") == 15
    scale = 1.0 / math.sqrt(16 * 2048)

    def one(j, _):
        group = block * GROUPS + j
        lanes = pl.ds(pl.multiple_of(j * LANES, LANES), LANES)
        raw, lag1, lag2, feat, cot = features(
            (q_ref, k_ref, v_ref), cot_ref, gath, prev, xs, lanes, group
        )
        for i in range(STEPS):
            us[i] = feat[1][i] * feat[2][i]
            gs[i] = cot[i] * feat[0][i]
            fs[0, i] = feat[1][i]
            fs[1, i] = feat[2][i]
        whole = own_rows(group, 0, MODES)
        rate = gath[own_rows(group, 32, MODES)]
        res = gath[whole]
        decay = jnp.exp(-rate)
        weights[0] = decay
        blocks = sub.astype(F32) * -16.0
        blocks_back = (7 - sub).astype(F32) * -16.0
        for base in range(0, MODES, 8):
            modes = range(base, base + 8)
            d = [spread(weights[0, m : m + 1, :]) for m in modes]
            r = [spread(gath[own_rows(group, m, 1)]) for m in modes]
            state, leave = [], []
            for m in modes:
                speed = spread(gath[own_rows(group, 32 + m, 1)])
                inner = jnp.where(sub > 0, pltpu.roll(ends[j, m], 1, 0), 0.0)
                state.append(inner + jnp.exp(speed * blocks) * spread(e_prior[own_rows(group, m, 1)]))
                inner = jnp.where(sub < 7, pltpu.roll(starts[j, m], 7, 0), 0.0)
                leave.append(inner + jnp.exp(speed * blocks_back) * spread(s_prior[own_rows(group, m, 1)]))
            res_sum = [jnp.zeros((8, LANES), F32)] * 8
            rate_sum = [jnp.zeros((8, LANES), F32)] * 8
            for n in range(8):
                hist[n, 0] = state[n]
            for i in range(STEPS):
                u, g = us[i], gs[i]
                total = None
                for n in range(8):
                    state[n] = d[n] * state[n] + u
                    if i + 1 < STEPS:
                        hist[n, i + 1] = state[n]
                    res_sum[n] = res_sum[n] + g * state[n]
                    term = r[n] * state[n]
                    total = term if total is None else total + term
                filt[i] = total if base == 0 else filt[i] + total
            for i in range(STEPS - 1, -1, -1):
                g = gs[i]
                total = None
                for n in range(8):
                    leave[n] = d[n] * leave[n] + g
                    rate_sum[n] = rate_sum[n] + leave[n] * hist[n, i]
                    term = r[n] * leave[n]
                    total = term if total is None else total + term
                back[i] = total if base == 0 else back[i] + total
            for n, m in enumerate(modes):
                grads[own_rows(group, m, 1)] = row_sum(res_sum[n]) * scale
                grads[own_rows(group, 32 + m, 1)] = (
                    row_sum(rate_sum[n]) * (d[n][:1] * r[n][:1]) * -scale
                )
        skip_row = gath[skip_place(group)]
        skip = spread(skip_row)

        taps = [[gath[tap_place(q, group, t)] for t in range(3)] for q in range(3)]
        after = []
        for q in range(3):
            x = [xs[q, 126:127, :], xs[q, 127:128, :],
                 nxt[pl.ds(q * 32 + group, 1), :], nxt[pl.ds(96 + q * 32 + group, 1), :]]
            after.append([taps[q][0] * x[t] + taps[q][1] * x[t - 1] + taps[q][2] * x[t - 2] for t in (2, 3)])
        next_cot = [nxt[pl.ds(192 + t * 32 + group, 1), :] for t in range(2)]
        next_mixed = [after[1][t] * after[2][t] for t in range(2)]
        next_grad = [next_cot[t] * after[0][t] for t in range(2)]
        state0 = decay * (e_in[whole] + jnp.exp(rate * -128.0) * e_prior[whole]) + next_mixed[0]
        state1 = decay * state0 + next_mixed[1]
        back0 = s_prior[whole]
        back1 = (back0 - next_grad[0]) * jnp.exp(rate)
        follow = [[], [], []]
        for t, (s, b) in enumerate(((state0, back0), (state1, back1))):
            filtered = row_sum(res * s) + skip_row * next_mixed[t]
            mixed = row_sum(res * b) + skip_row * next_grad[t]
            follow[0].append(next_cot[t] * filtered)
            follow[1].append(mixed * after[2][t])
            follow[2].append(mixed * after[1][t])

        skip_sum = jnp.zeros((8, LANES), F32)
        grad = [[], [], []]
        for i in range(STEPS):
            u, g = us[i], gs[i]
            skip_sum = skip_sum + u * g
            mixed = back[i] + skip * g
            grad[0].append(xs[3, pl.ds(i, 8, stride=STEPS), :] * (filt[i] + skip * u))
            grad[1].append(mixed * fs[1, i])
            grad[2].append(mixed * fs[0, i])
        grads[skip_place(group)] = row_sum(skip_sum) * scale
        grads[group // 2, 84:96, :] = jnp.zeros((12, LANES), F32)
        for q in range(3):
            t = [spread(taps[q][k]) for k in range(3)]
            tail = []
            for k in range(2):
                row = jnp.where(edge, 0.0, follow[q][k])
                tail.append(jnp.where(sub == 7, spread(row), pltpu.roll(grad[q][k], 7, 0)))
            g = grad[q] + tail
            sums = [jnp.zeros((8, LANES), F32)] * 3
            for i in range(STEPS):
                sums[0] = sums[0] + raw[q][i] * g[i]
                sums[1] = sums[1] + lag1[q][i] * g[i]
                sums[2] = sums[2] + lag2[q][i] * g[i]
            for i in range(STEPS):
                xs[q, pl.ds(i, 8, stride=STEPS), :] = t[0] * g[i] + t[1] * g[i + 1] + t[2] * g[i + 2]
            for k in range(3):
                grads[tap_place(q, group, k)] = row_sum(sums[k]) * scale
            out[0, :, pl.ds(pl.multiple_of((q * 32 + group) * LANES, LANES), LANES)] = (
                xs[q].astype(jnp.bfloat16)
            )
        return 0

    lax.fori_loop(0, GROUPS, one, 0)


def reduce_kernel(part, out, chip, near, acc, shares, mine, sums, half,
                  s1, r1, s2, r2, s3, r3, s4, r4):
    p, f, c, _, _ = place()
    partner = p + 1 - 2 * c
    for step in range(1, OWNERS):
        greet(p, (f + step) % OWNERS)
    greet(partner, f)
    for step in range(1, 8):
        greet((p + 2 * step) % 16, f)
    pl.semaphore_wait(pltpu.get_barrier_semaphore(), 23)

    keep = pl.multiple_of(c * HALF, 8)
    give = pl.multiple_of(HALF - c * HALF, 8)
    pair = remote(part.at[:, pl.ds(give, HALF)], near, s1, r1, partner, f)
    pair.start()
    pair.wait_recv()
    out_copies = []
    acc[...] = part[:, pl.ds(keep, HALF), :] + near[...]
    for step in range(1, OWNERS):
        to = (f + step) % OWNERS
        copy = remote(acc.at[to], shares.at[f], s2.at[step], r2.at[step], p, to)
        copy.start()
        out_copies.append(copy)
    shares[f] = acc[f]
    for step in range(1, OWNERS):
        source = (f + OWNERS - step) % OWNERS
        remote(acc.at[f], shares.at[source], s2.at[step], r2.at[step], p, f).wait_recv()
    total = shares[0]
    for k in range(1, OWNERS):
        total = total + shares[k]
    me = p // 2
    sums[me] = total
    for step in range(1, 8):
        copy = remote(sums.at[me], sums.at[me], s3.at[step], r3.at[step], (p + 2 * step) % 16, f)
        copy.start()
        out_copies.append(copy)
    for step in range(1, 8):
        source = (me + 8 - step) % 8
        remote(sums.at[source], sums.at[source], s3.at[step], r3.at[step], p, f).wait_recv()
    total = sums[0]
    for k in range(1, 8):
        total = total + sums[k]
    out[pl.ds(keep, HALF), :] = total
    mine_ref = out.at[pl.ds(keep, HALF)]
    back = remote(mine_ref, mine_ref, s4, r4, partner, f)
    back.start()
    other = out.at[pl.ds(give, HALF)]
    remote(other, other, s4, r4, partner, f).wait_recv()
    back.wait_send()
    pair.wait_send()
    for copy in out_copies:
        copy.wait_send()


def shape(*dims, dtype=F32):
    return jax.ShapeDtypeStruct(dims, dtype)


def params(ident=None, limit=48):
    extra = {} if ident is None else {"collective_id": ident, "has_side_effects": True}
    return pltpu.CompilerParams(vmem_limit_bytes=limit * 2**20, **extra)


def per_device(rows_in, cotangent, taps, residues, rates, skip, state_before, adjoint_after):
    dma = pltpu.SemaphoreType.DMA
    bf16 = jnp.bfloat16
    tail = rows_in[0, 126:128].reshape(192, LANES)
    head = jnp.concatenate(
        [rows_in[0, 0:2].reshape(192, LANES), cotangent[0, 0:2].reshape(64, LANES)], axis=0
    )
    gath, prev, nxt = pl.pallas_call(
        gather_kernel,
        out_shape=(shape(OWNERS, ROWS, LANES), shape(192, LANES), shape(256, LANES)),
        in_specs=[VMEM] * 6,
        out_specs=(VMEM,) * 3,
        scratch_shapes=[
            pltpu.VMEM((192, LANES), bf16), pltpu.VMEM((256, LANES), bf16),
            dma((16,)), dma((16,)), dma((16,)), dma((16,)), dma((2,)), dma((2,)),
        ],
        compiler_params=params(1),
        name="gather",
    )(residues, rates, taps, skip[None, :], tail, head)

    width = GROUPS * LANES

    def section(q):
        return pl.BlockSpec((1, 128, width), lambda b, q=q: (0, 0, q * GRID + b))

    def fixed(*dims):
        return pl.BlockSpec(dims, lambda b: (0,) * len(dims))

    inner = pl.BlockSpec((GROUPS, MODES, 8, LANES), lambda b: (b, 0, 0, 0))
    small = (OWNERS, 2 * MODES, LANES)
    ends, starts, e_all, s_all = pl.pallas_call(
        local_kernel,
        grid=(GRID,),
        out_shape=(shape(32, MODES, 8, LANES), shape(32, MODES, 8, LANES), shape(*small), shape(*small)),
        in_specs=[section(0), section(1), section(2), section(0),
                  fixed(OWNERS, ROWS, LANES), fixed(192, LANES)],
        out_specs=(inner, inner, fixed(*small), fixed(*small)),
        scratch_shapes=[
            pltpu.VMEM((4, 128, LANES), F32), pltpu.VMEM((STEPS, 8, LANES), F32),
            pltpu.VMEM((STEPS, 8, LANES), F32), pltpu.VMEM((4, MODES, LANES), F32),
        ],
        compiler_params=params(),
        name="local",
    )(rows_in, rows_in, rows_in, cotangent, gath, prev)

    buf = pltpu.VMEM(small, F32)
    e_prior, s_prior = pl.pallas_call(
        prefix_kernel,
        out_shape=(shape(*small), shape(*small)),
        in_specs=[VMEM] * 5,
        out_specs=(VMEM,) * 2,
        scratch_shapes=[
            buf, buf, pltpu.VMEM((3,) + small, F32), buf, buf, buf, buf, buf, buf,
            dma((PARTS,)), dma((PARTS,)), dma((PARTS,)), dma((PARTS,)),
            dma((3, PARTS)), dma((3, PARTS)), dma((PARTS,)), dma((PARTS,)), dma((PARTS,)), dma((PARTS,)),
        ],
        compiler_params=params(2),
        name="prefix",
    )(e_all, s_all, gath, state_before, adjoint_after)

    vec = pltpu.VMEM((STEPS, 8, LANES), F32)
    grad_rows, grads = pl.pallas_call(
        main_kernel,
        grid=(GRID,),
        out_shape=(shape(1, 128, 12288, dtype=bf16), shape(OWNERS, ROWS, LANES)),
        in_specs=[section(0), section(1), section(2), section(0),
                  fixed(OWNERS, ROWS, LANES), fixed(192, LANES), fixed(256, LANES), inner, inner,
                  fixed(*small), fixed(*small), fixed(*small)],
        out_specs=(fixed(1, 128, 12288), fixed(OWNERS, ROWS, LANES)),
        scratch_shapes=[
            pltpu.VMEM((4, 128, LANES), F32), vec, vec, pltpu.VMEM((2, STEPS, 8, LANES), F32),
            pltpu.VMEM((8, STEPS, 8, LANES), F32), vec, vec, pltpu.VMEM((1, MODES, LANES), F32),
        ],
        compiler_params=params(),
        name="main",
    )(rows_in, rows_in, rows_in, cotangent, gath, prev, nxt, ends, starts, e_all, e_prior, s_prior)

    part = pltpu.VMEM((OWNERS, HALF, LANES), F32)
    total = pl.pallas_call(
        reduce_kernel,
        out_shape=shape(ROWS, LANES),
        in_specs=[VMEM],
        out_specs=VMEM,
        scratch_shapes=[
            part, part, part, part, part, pltpu.VMEM((8, HALF, LANES), F32), part,
            dma(()), dma(()), dma((16,)), dma((16,)), dma((8,)), dma((8,)), dma(()), dma(()),
        ],
        compiler_params=params(3),
        name="reduce",
    )(grads)
    return (
        grad_rows,
        total[64:82].reshape(3, 768),
        jnp.concatenate([total[0:16], total[16:32]], axis=1),
        jnp.concatenate([total[32:48], total[48:64]], axis=1),
        total[82:84].reshape(256),
    )


def solution(mesh):
    in_specs = (
        P("fsdp", "ctx", None),
        P("fsdp", "ctx", None),
        P(None, "fsdp"),
        P(None, "fsdp"),
        P(None, "fsdp"),
        P("fsdp"),
        P("fsdp", None, None),
        P("fsdp", None, None),
    )
    out_specs = (
        P("fsdp", "ctx", None),
        P(None, "fsdp"),
        P(None, "fsdp"),
        P(None, "fsdp"),
        P("fsdp"),
    )
    return jax.shard_map(
        per_device, mesh=mesh, in_specs=in_specs, out_specs=out_specs, check_vma=False
    )
```

time: 965 us -> 125 us (0.13)
  waiting for transfers between devices: 473 us -> 0 us
  blocking collectives: 235 us -> 0 us
  other arithmetic: 157 us -> 0.62 us
  Pallas kernels: 0 us -> 116 us
  local copies, waits for them, and re-layouts: 63 us -> 7.3 us
  between operations: 16.2 us -> 0.71 us
  starting transfers between devices: 14.1 us -> 0 us
    unnamed x9 -> x0, waiting for transfers between devices: 206 us -> none
    reduce_scatter x2 -> x0, waiting for transfers between devices: 154 us -> none  [the longest x1 82.6 us: per_device(): lax.psum_scatter(res_terms, 'fsdp', scatter_dimension=1, tiled=True)]
    all_gather x4 -> x0, blocking collectives: 145 us -> none  [the longest x1 40 us: per_device(): lax.all_gather(residues, 'fsdp', axis=1, tiled=True)]
    pallas_call x0 -> x5, Pallas kernels: none -> 116 us  [the longest x1 32.9 us: per_device(): pl.pallas_call(reduce_kernel, out_shape=shape(ROWS, LANES), in_specs=[VME...]
    all_gather x3 -> x0, waiting for transfers between devices: 109 us -> none  [prefix(): gathered = jax.tree.map(lambda a: lax.all_gather(a, axis), part)]
    psum x1 -> x0, blocking collectives: 90.1 us -> none  [per_device(): totals = lax.psum((shares[0], shares[1], shares[2], shares[3]), 'ctx')]
    add x32 -> x0, other arithmetic: 65.3 us -> none  [the longest x21 23.5 us: link(): return (first[0] * second[0], second[0] * first[1] + second[1])]
    reduce_sum x7 -> x0, other arithmetic: 58.3 us -> none  [the longest x1 14.8 us: per_device(): jnp.sum(mixed_blocks[:, :, :, None, :] * (reverse_powers * (width - 1.0 -...]
  transfers between devices with their start and end apart: 9 -> 0, of which waited for: 7 -> 0; matrix products, arithmetic and copies ran while one was open for 15% -> 0% of each run, Pallas kernels for 0% -> 0%
where the time goes in v1:
time: 125 us; the launch traced here: 124 us
  Pallas kernels  116 us (93%)
  local copies, waits for them, and re-layouts  7.3 us (6%)
    pallas_call x1, Pallas kernels, per_device(): pl.pallas_call(reduce_kernel, out_shape=shape(ROWS, LANES), in_specs=[VME...  32.9 us
    pallas_call x1, Pallas kernels, per_device(): pl.pallas_call(main_kernel, grid=(GRID,), out_shape=(shape(1, 128, 12288,...  27.5 us
    pallas_call x1, Pallas kernels, per_device(): pl.pallas_call(gather_kernel, out_shape=(shape(OWNERS, ROWS, LANES), shap...  24 us
    pallas_call x1, Pallas kernels, per_device(): pl.pallas_call(prefix_kernel, out_shape=(shape(*small), shape(*small)), i...  19.4 us
    pallas_call x1, Pallas kernels, per_device(): pl.pallas_call(local_kernel, grid=(GRID,), out_shape=(shape(32, MODES, 8,...  11.9 us
    unnamed x16, local copies, waits for them, and re-layouts  4.05 us

profile of v1, /device:TPU:1, one launch (start us, length us, event | category | flops | bytes accessed | tf_op | source)
XLA Modules:
  0.0 124.4 jit_solution(15874705491396570946)
XLA Ops:
  0.6 0.9 slice.29
  1.5 1.1 fusion
  2.7 0.0 copy-start.4
  2.7 0.7 copy-done.4
  3.5 0.0 copy-start.5
  3.5 0.7 copy-done.5
  4.2 0.0 copy-start.6
  4.2 0.7 copy-done.6
  4.9 0.0 copy-start.7
  4.9 0.7 copy-done.7
  5.6 24.0 %gather.1 = (f32[16,96,128]{2,1,0:T(8,128)S(1)}, f32[192,128]{1,0:T(8,128)S(1)}, f32[256,128]{1,0:T(8,128)S(1)}) custom-call(f32[16,256]{1,0:T(8,128)S(1)} %copy-done.4, f32[16,256]{1,0:T(8,128)S(1)} %copy-done.5, f32[3,768]{1,0:T(4,128)S(1)} %copy-done.6, f32[1,256]{1,0:T(1,128)S(1)} %bitcast.3, bf16[192,128]{1,0:T(8,128)(2,1)S(1)} %reshape_squeeze.9.tail, ...), custom_call_target="tpu_custom_call" | custom-call | tf_op jit(solution)/shard_map/gather/pallas_call | solution.py:543
  29.6 0.0 copy-start
  29.6 1.2 copy-done
  30.8 0.0 copy-start.2
  30.8 0.0 copy-start.3
  30.8 0.0 copy-start.1
  30.8 11.9 %local.1 = (f32[32,16,8,128]{3,2,1,0:T(8,128)S(1)}, f32[32,16,8,128]{3,2,1,0:T(8,128)}, f32[16,32,128]{2,1,0:T(8,128)S(1)}, f32[16,32,128]{2,1,0:T(8,128)S(1)}) custom-call(bf16[1,128,12288]{2,1,0:T(8,128)(2,1)} %v_ref.3, bf16[1,128,12288]{2,1,0:T(8,128)(2,1)} %v_ref.3, bf16[1,128,12288]{2,1,0:T(8,128)(2,1)} %v_ref.3, bf16[1,128,4096]{2,1,0:T(8,128)(2,1)S(1)} %copy-done, ...), custom_call_target="tpu_custom_call" | custom-call | tf_op jit(solution)/shard_map/local/pallas_call | solution.py:566
  42.8 0.0 copy-done.2
  42.8 0.0 copy-done.3
  42.8 19.4 %prefix.1 = (f32[16,32,128]{2,1,0:T(8,128)S(1)}, f32[16,32,128]{2,1,0:T(8,128)S(1)}) custom-call(f32[16,32,128]{2,1,0:T(8,128)S(1)} %get-tuple-element.21.e_in, f32[16,32,128]{2,1,0:T(8,128)S(1)} %get-tuple-element.22.s_in, f32[16,96,128]{2,1,0:T(8,128)S(1)} %get-tuple-element.16.gath, f32[1,16,4096]{2,1,0:T(8,128)S(1)} %copy-done.2, ...), custom_call_target="tpu_custom_call" | custom-call | tf_op jit(solution)/shard_map/prefix/pallas_call | solution.py:582
  62.2 0.0 copy-done.1
  62.2 27.5 %main.1 = (bf16[1,128,12288]{2,1,0:T(8,128)(2,1)}, f32[16,96,128]{2,1,0:T(8,128)S(1)}) custom-call(bf16[1,128,12288]{2,1,0:T(8,128)(2,1)} %v_ref.3, bf16[1,128,12288]{2,1,0:T(8,128)(2,1)} %v_ref.3, bf16[1,128,12288]{2,1,0:T(8,128)(2,1)} %v_ref.3, bf16[1,128,4096]{2,1,0:T(8,128)(2,1)S(1)} %copy-done.1, f32[16,96,128]{2,1,0:T(8,128)S(1)} %get-tuple-element.16.gath, ...), custom_call_target="tpu_custom_call" | custom-call | tf_op jit(solution)/shard_map/main/pallas_call | solution.py:597
  89.6 32.9 %reduce.1 = f32[96,128]{1,0:T(8,128)S(1)} custom-call(f32[16,96,128]{2,1,0:T(8,128)S(1)} %get-tuple-element.26.part), custom_call_target="tpu_custom_call" | custom-call | tf_op jit(solution)/shard_map/reduce/pallas_call | solution.py:614
  122.6 0.6 slice_bitcast_fusion
  123.2 0.6 reshape.16
  123.8 0.6 pad_maximum_fusion.1
  (6 shorter events, 0.1 us)
Async XLA Ops:
  2.7 0.7 copy-start.4
  3.5 0.7 copy-start.5
  4.2 0.7 copy-start.6
  4.9 0.7 copy-start.7
  29.6 1.2 copy-start
  30.8 12.0 %copy-start.2 = (f32[1,16,4096]{2,1,0:T(8,128)S(1)}, f32[1,16,4096]{2,1,0:T(8,128)}, u32[]{:S(2)}) copy-start(f32[1,16,4096]{2,1,0:T(8,128)} %before.1) | copy-start | bytes 786436
  30.8 12.0 %copy-start.3 = (f32[1,16,4096]{2,1,0:T(8,128)S(1)}, f32[1,16,4096]{2,1,0:T(8,128)}, u32[]{:S(2)}) copy-start(f32[1,16,4096]{2,1,0:T(8,128)} %after.1) | copy-start | bytes 786436
  30.8 31.3 %copy-start.1 = (bf16[1,128,4096]{2,1,0:T(8,128)(2,1)S(1)}, bf16[1,128,4096]{2,1,0:T(8,128)(2,1)}, u32[]{:S(2)}) copy-start(bf16[1,128,4096]{2,1,0:T(8,128)(2,1)} %cot_ref.3) | copy-start | bytes 3145732

commit v2 on v0

v2 whole, which is shorter than its diff:
```python
import math

import jax
import jax.numpy as jnp
from jax import lax
from jax.experimental import pallas as pl
from jax.experimental.pallas import tpu as pltpu
from jax.sharding import PartitionSpec as P

MESH = pl.DeviceIdType.MESH
F32 = jnp.float32
BF16 = jnp.bfloat16
MODES = 16
LANES = 128
STEPS = 16
OWNERS = 16
ROWS = 88
MODAL = 64
REST = ROWS - MODAL
WIDTH = 8
AHEAD = 4
STAGE1, STAGE2, STAGE3, STAGE4, STAGE5 = 1, 7, 10, 16, 17
MAIN = STAGE5 + 1
TURNS = MAIN + OWNERS
VMEM = pl.BlockSpec(memory_space=pltpu.VMEM)
ANY = pl.BlockSpec(memory_space=pl.ANY)


def remote(src, dst, send, recv, ctx, fsdp):
    return pltpu.make_async_remote_copy(
        src_ref=src, dst_ref=dst, send_sem=send, recv_sem=recv,
        device_id=(ctx, fsdp), device_id_type=MESH,
    )


def greet(ctx, fsdp):
    pl.semaphore_signal(
        pltpu.get_barrier_semaphore(), inc=1, device_id=(ctx, fsdp), device_id_type=MESH
    )


def spread(row):
    return jnp.broadcast_to(row, (8, LANES))


def spread_rows(rows):
    return jnp.broadcast_to(rows[:, None, :], (rows.shape[0], 8, LANES))


def sublane():
    return lax.broadcasted_iota(jnp.int32, (8, LANES), 0)


def row_sum(x):
    return jnp.sum(x, axis=0, keepdims=True)


def tree(terms):
    count = terms.shape[0]
    while count > 1:
        count //= 2
        terms = terms[:count] + terms[count:]
    return terms[0]


def tap_place(section, group, j):
    unit = section * 32 + group
    return unit // 6, pl.ds(MODAL + 6 * j + unit % 6, 1)


def own_rows(group, first, count):
    base = (group % 2) * MODES
    if count % 8 == 0:
        base = pl.multiple_of(base, MODES)
    return group // 2, pl.ds(base + first, count)


def lanes_of(unit, count=1):
    return pl.ds(pl.multiple_of(unit * LANES, LANES), count * LANES)


def local_pass(group, rows, cot, gath, prev, xs, X, F, U, G, C, ends, starts, e_all, s_all, weights):
    sub = sublane()
    top = sub == 0
    feat = []
    for q in range(3):
        unit = q * 32 + group
        xs[...] = rows[0, :, lanes_of(unit)].astype(F32)
        for i in range(STEPS):
            X[group, q, 2 + i] = xs[pl.ds(i, 8, stride=STEPS), :]
        near = spread(prev[pl.ds(96 + unit, 1), :])
        far = spread(prev[pl.ds(unit, 1), :])
        X[group, q, 1] = jnp.where(top, near, pltpu.roll(X[group, q, 17], 1, 0))
        X[group, q, 0] = jnp.where(top, far, pltpu.roll(X[group, q, 16], 1, 0))
        t = [spread(gath[tap_place(q, group, j)]) for j in range(3)]
        feat.append(t[0] * X[group, q, 2:18] + t[1] * X[group, q, 1:17] + t[2] * X[group, q, 0:16])
        if q:
            F[group, q - 1] = feat[q]
    xs[...] = cot[0, :, lanes_of(group)].astype(F32)
    for i in range(STEPS):
        C[group, i] = xs[pl.ds(i, 8, stride=STEPS), :]
    U[group] = feat[1] * feat[2]
    G[group] = C[group] * feat[0]
    rate = gath[own_rows(group, 32, MODES)]
    weights[0] = jnp.exp(-rate)
    weights[1] = jnp.exp(-16.0 * rate)
    weights[2] = jnp.exp(-32.0 * rate)
    weights[3] = jnp.exp(-64.0 * rate)
    d = spread_rows(weights[0])
    e = jnp.broadcast_to(U[group, 0], (MODES, 8, LANES))
    b = jnp.broadcast_to(G[group, 15], (MODES, 8, LANES))
    for i in range(1, STEPS):
        e = d * e + U[group, i]
        b = d * b + G[group, 15 - i]
    for power, shift in ((1, 1), (2, 2), (3, 4)):
        w = spread_rows(weights[power])
        e = e + jnp.where(sub >= shift, w, 0.0) * pltpu.roll(e, shift, 1)
        b = b + jnp.where(sub < 8 - shift, w, 0.0) * pltpu.roll(b, 8 - shift, 1)
    ends[group] = e
    starts[group] = b
    for n in range(MODES):
        e_all[own_rows(group, n, 1)] = e[n, 7:8]
        s_all[own_rows(group, n, 1)] = b[n, 0:1]


def main_pass(group, edge, gath, nxt, xs, X, F, U, G, C, ends, starts, e_all, e_prior, s_prior,
              out, grads, hist, filt, back, GB, weights):
    sub = sublane()
    scale = 1.0 / math.sqrt(16 * 2048)
    whole = own_rows(group, 0, MODES)
    rate = gath[own_rows(group, 32, MODES)]
    res = gath[whole]
    decay = jnp.exp(-rate)
    weights[0] = decay
    blocks = sub.astype(F32) * -16.0
    blocks_back = (7 - sub).astype(F32) * -16.0
    for base in range(0, MODES, WIDTH):
        some = slice(base, base + WIDTH)
        here = own_rows(group, base, WIDTH)
        d = spread_rows(weights[0, some])
        r = spread_rows(gath[here])
        speed = spread_rows(gath[own_rows(group, 32 + base, WIDTH)])
        state = jnp.where(sub > 0, pltpu.roll(ends[group, some], 1, 1), 0.0)
        state = state + jnp.exp(speed * blocks) * spread_rows(e_prior[here])
        leave = jnp.where(sub < 7, pltpu.roll(starts[group, some], 7, 1), 0.0)
        leave = leave + jnp.exp(speed * blocks_back) * spread_rows(s_prior[here])
        hist[0] = state
        res_sum = jnp.zeros((WIDTH, 8, LANES), F32)
        rate_sum = res_sum
        for i in range(STEPS):
            state = d * state + U[group, i]
            if i + 1 < STEPS:
                hist[i + 1] = state
            res_sum = res_sum + G[group, i] * state
            total = tree(r * state)
            filt[i] = total if base == 0 else filt[i] + total
        for i in range(STEPS - 1, -1, -1):
            leave = d * leave + G[group, i]
            rate_sum = rate_sum + leave * hist[i]
            total = tree(r * leave)
            back[i] = total if base == 0 else back[i] + total
        grads[here] = jnp.sum(res_sum, axis=1) * scale
        grads[own_rows(group, 32 + base, WIDTH)] = (
            jnp.sum(rate_sum, axis=1) * (weights[0, some] * gath[here]) * -scale
        )
    skip_at = (group // 2, pl.ds(82 + group % 2, 1))
    skip_row = gath[skip_at]
    skip = spread(skip_row)

    taps = [[gath[tap_place(q, group, t)] for t in range(3)] for q in range(3)]
    after = []
    for q in range(3):
        unit = q * 32 + group
        x = [X[group, q, 16, 7:8], X[group, q, 17, 7:8],
             nxt[pl.ds(unit, 1), :], nxt[pl.ds(96 + unit, 1), :]]
        after.append([taps[q][0] * x[t] + taps[q][1] * x[t - 1] + taps[q][2] * x[t - 2] for t in (2, 3)])
    next_cot = [nxt[pl.ds(192 + t * 32 + group, 1), :] for t in range(2)]
    next_mixed = [after[1][t] * after[2][t] for t in range(2)]
    next_grad = [next_cot[t] * after[0][t] for t in range(2)]
    state0 = decay * (e_all[whole] + jnp.exp(rate * -128.0) * e_prior[whole]) + next_mixed[0]
    state1 = decay * state0 + next_mixed[1]
    back0 = s_prior[whole]
    back1 = (back0 - next_grad[0]) * jnp.exp(rate)
    follow = [[], [], []]
    for t, (s, b) in enumerate(((state0, back0), (state1, back1))):
        filtered = row_sum(res * s) + skip_row * next_mixed[t]
        mixed = row_sum(res * b) + skip_row * next_grad[t]
        follow[0].append(next_cot[t] * filtered)
        follow[1].append(mixed * after[2][t])
        follow[2].append(mixed * after[1][t])

    u, g = U[group], G[group]
    grads[skip_at] = row_sum(jnp.sum(u * g, axis=0)) * scale
    mixed = back[...] + skip * g
    GB[0, 0:16] = C[group] * (filt[...] + skip * u)
    GB[1, 0:16] = mixed * F[group, 1]
    GB[2, 0:16] = mixed * F[group, 0]
    for q in range(3):
        t = [spread(taps[q][k]) for k in range(3)]
        for k in range(2):
            row = jnp.where(edge, 0.0, follow[q][k])
            GB[q, 16 + k] = jnp.where(sub == 7, spread(row), pltpu.roll(GB[q, k], 7, 0))
        grad = GB[q, 0:16]
        for k in range(3):
            terms = X[group, q, 2 - k : 18 - k] * grad
            grads[tap_place(q, group, k)] = row_sum(jnp.sum(terms, axis=0)) * scale
        y = t[0] * grad + t[1] * GB[q, 1:17] + t[2] * GB[q, 2:18]
        for i in range(STEPS):
            xs[pl.ds(i, 8, stride=STEPS), :] = y[i]
        out[0, :, lanes_of(q * 32 + group)] = xs[...].astype(BF16)


def kernel(rows_hbm, cot_hbm, taps, residues, rates, skip, before, after, rows_out, result,
           rows, cot, out, gath, grads, prev, nxt, tail_f, head_f, tail_b, head_b, prev_b, next_b,
           xs, X, F, U, G, C, ends, starts, e_all, s_all, e_prior, s_prior, hist, filt, back, GB, weights,
           first, second, third, whole, last, agg, chip, begin, inner,
           shares, shares_rest, sums, sums_rest, mine, other,
           in_sem, out_sem, halo_s, halo_r, rest_s, rest_r, modal_s, modal_r, hand_s, hand_r,
           s1, r1, s2, r2, s3, r3, s4, r4, s5, r5,
           share_s, share_r, share2_s, share2_r, sum_s, sum_r, sum2_s, sum2_r, end_s, end_r):
    p = lax.axis_index("ctx")
    f = lax.axis_index("fsdp")
    c, h, x = p % 2, (p // 2) % 2, p // 4
    partner = p + 1 - 2 * c
    across = p + 2 - 4 * h
    resident = h == c
    n = jnp.where(c == 1, x, 3 - x)
    sign = jnp.where(c == 1, 4, -4)
    edge = p == 15

    load_rows = pltpu.make_async_copy(rows_hbm, rows, in_sem.at[0])
    load_cot = pltpu.make_async_copy(cot_hbm, cot, in_sem.at[1])
    load_rows.start()
    load_cot.start()
    for step in range(1, OWNERS):
        greet(p, (f + step) % OWNERS)
    for step in range(1, 8):
        greet((p + 2 * step) % 16, f)
    greet(partner, f)
    greet((p + 15 + 2 * c) % 16, f)

    for b in range(2):
        cols = slice(LANES * b, LANES * (b + 1))
        gath[f, 16 * b : 16 * (b + 1), :] = residues[:, cols]
        gath[f, 32 + 16 * b : 48 + 16 * b, :] = rates[:, cols]
        gath[f, 82 + b : 83 + b, :] = skip[:, cols]
    for j in range(3):
        for b in range(6):
            row = MODAL + 6 * j + b
            gath[f, row : row + 1, :] = taps[j : j + 1, LANES * b : LANES * (b + 1)]
    gath[f, 84:88, :] = jnp.zeros((4, LANES), F32)
    for o in range(OWNERS):
        grads[o, 84:88, :] = jnp.zeros((4, LANES), F32)

    load_rows.wait()
    load_cot.wait()

    def edges(unit, _):
        end = rows[0, 112:128, lanes_of(unit)].astype(F32)
        tail_f[pl.ds(unit, 1), :] = end[14:15]
        tail_f[pl.ds(96 + unit, 1), :] = end[15:16]
        start = rows[0, 0:16, lanes_of(unit)].astype(F32)
        head_f[pl.ds(unit, 1), :] = start[0:1]
        head_f[pl.ds(96 + unit, 1), :] = start[1:2]
        return 0

    def edges_cot(unit, _):
        start = cot[0, 0:16, lanes_of(unit)].astype(F32)
        head_f[pl.ds(192 + unit, 1), :] = start[0:1]
        head_f[pl.ds(224 + unit, 1), :] = start[1:2]
        return 0

    lax.fori_loop(0, 96, edges, 0)
    lax.fori_loop(0, 32, edges_cot, 0)
    tail_b[...] = tail_f[...].astype(BF16)
    head_b[...] = head_f[...].astype(BF16)
    pl.semaphore_wait(pltpu.get_barrier_semaphore(), 24)

    right = remote(tail_b, prev_b, halo_s.at[0], halo_r.at[0], p + 1, f)
    left = remote(head_b, next_b, halo_s.at[1], halo_r.at[1], p - 1, f)

    @pl.when(p < 15)
    def _():
        right.start()

    @pl.when(p > 0)
    def _():
        left.start()

    def rest_copy(step, owner, to):
        block = gath.at[owner, pl.ds(MODAL, REST)]
        return remote(block, block, rest_s.at[step], rest_r.at[step], p, to)

    part = pl.multiple_of(32 - 32 * c, 32)
    part_other = pl.multiple_of(32 * c, 32)

    def modal_copy(step, owner, to):
        block = gath.at[owner, pl.ds(part, 32)]
        return remote(block, block, modal_s.at[step], modal_r.at[step], p, to)

    def hand_copy(step, rows_from):
        block = gath.at[(f + step) % OWNERS, pl.ds(rows_from, 32)]
        return remote(block, block, hand_s.at[step], hand_r.at[step], partner, f)

    for step in range(1, OWNERS):
        rest_copy(step, f, (f + OWNERS - step) % OWNERS).start()
    for step in range(1, OWNERS):
        modal_copy(step, f, (f + OWNERS - step) % OWNERS).start()

    @pl.when(p > 0)
    def _():
        right.wait_recv()
        prev[...] = prev_b[...].astype(F32)

    @pl.when(p == 0)
    def _():
        prev[...] = jnp.zeros_like(prev)

    @pl.when(p < 15)
    def _():
        left.wait_recv()
        nxt[...] = next_b[...].astype(F32)

    @pl.when(p == 15)
    def _():
        nxt[...] = jnp.zeros_like(nxt)

    for step in range(1, OWNERS):
        rest_copy(step, (f + step) % OWNERS, f).wait_recv()

    def hand_on(step):
        modal_copy(step, (f + step) % OWNERS, f).wait_recv()
        hand_copy(step, part).start()

    for step in range(1, 1 + AHEAD):
        hand_on(step)

    def copy1(o, ref):
        return remote(ref.at[o], first.at[o], s1.at[o], r1.at[o], partner, f)

    def copy2(o):
        return remote(agg.at[o], second.at[o], s2.at[o], r2.at[o], across, f)

    def copy3(o, j):
        return remote(chip.at[o], third.at[j - 1, o], s3.at[j - 1, o], r3.at[j - 1, o], p + sign * j, f)

    def copy4(o):
        return remote(begin.at[o], whole.at[o], s4.at[o], r4.at[o], across, f)

    def copy5(o, ref):
        return remote(ref.at[o], last.at[o], s5.at[o], r5.at[o], partner, f)

    def decay(o, power):
        return jnp.exp(gath[o, 32:64, :] * (-128.0 * power))

    def stage1(o):
        copy1(o, e_all).wait_recv()
        own = jnp.where(c == 1, e_all[o], s_all[o])
        agg[o] = own + decay(o, 1) * first[o]

        @pl.when(jnp.logical_not(resident))
        def _():
            copy2(o).start()

    def stage2(o):
        @pl.when(resident)
        def _():
            copy2(o).wait_recv()
            chip[o] = agg[o] + decay(o, 2) * second[o]
            for j in range(1, 4):
                @pl.when(n + j < 4)
                def _():
                    copy3(o, j).start()

    def own_prior(o, value):
        @pl.when(c == 1)
        def _():
            e_prior[o] = value

        @pl.when(c == 0)
        def _():
            s_prior[o] = value

    def stage3(o):
        @pl.when(resident)
        def _():
            for b in range(2):
                cols = lanes_of(2 * o + b)
                begin[o, 16 * b : 16 * (b + 1), :] = jnp.where(c == 1, before[0, :, cols], after[0, :, cols])
            span = decay(o, 4)
            for j in range(3, 0, -1):
                @pl.when(n >= j)
                def _():
                    copy3(o, j).wait_recv()
                    begin[o] = third[j - 1, o] + span * begin[o]
            copy4(o).start()
            inner[o] = decay(o, 2) * begin[o] + second[o]
            copy5(o, inner).start()
            own_prior(o, decay(o, 1) * inner[o] + first[o])

    def stage4(o):
        @pl.when(jnp.logical_not(resident))
        def _():
            copy4(o).wait_recv()
            copy5(o, whole).start()
            own_prior(o, decay(o, 1) * whole[o] + first[o])

    def stage5(o):
        copy5(o, whole).wait_recv()

        @pl.when(c == 1)
        def _():
            s_prior[o] = last[o]

        @pl.when(c == 0)
        def _():
            e_prior[o] = last[o]

    def share_copy(source, to):
        return remote(grads.at[to, pl.ds(0, MODAL)], shares.at[source],
                      share_s.at[to], share_r.at[source], p, to)

    def rest_share(source, to):
        return remote(grads.at[to, pl.ds(MODAL, REST)], shares_rest.at[source],
                      share2_s.at[to], share2_r.at[source], p, to)

    def out_copy(o, q):
        block = (slice(None), slice(None), lanes_of(q * 32 + 2 * o, 2))
        return pltpu.make_async_copy(out.at[block], rows_out.at[block], out_sem.at[q, o])

    def turn(t, _):
        @pl.when(t < OWNERS)
        def _():
            @pl.when(t + AHEAD + 1 < OWNERS)
            def _():
                hand_on(t + AHEAD + 1)

            @pl.when(t > 0)
            def _():
                hand_copy(t, part_other).wait_recv()
            o = (f + t) % OWNERS

            def one(j, _):
                local_pass(2 * o + j, rows, cot, gath, prev, xs, X, F, U, G, C, ends, starts,
                           e_all, s_all, weights)
                return 0

            lax.fori_loop(0, 2, one, 0)

            @pl.when(c == 0)
            def _():
                copy1(o, e_all).start()

            @pl.when(c == 1)
            def _():
                copy1(o, s_all).start()

        for stage, lag in ((stage5, STAGE5), (stage4, STAGE4), (stage3, STAGE3), (stage2, STAGE2),
                           (stage1, STAGE1)):
            @pl.when(jnp.logical_and(t >= lag, t < lag + OWNERS))
            def _():
                stage((f + t - lag) % OWNERS)

        @pl.when(t >= MAIN)
        def _():
            o = (f + t - MAIN + 1) % OWNERS

            def one(j, _):
                main_pass(2 * o + j, edge, gath, nxt, xs, X, F, U, G, C, ends, starts, e_all,
                          e_prior, s_prior, out, grads, hist, filt, back, GB, weights)
                return 0

            lax.fori_loop(0, 2, one, 0)
            for q in range(3):
                out_copy(o, q).start()

            @pl.when(t < TURNS - 1)
            def _():
                share_copy(f, o).start()

        return 0

    lax.fori_loop(0, TURNS, turn, 0)

    for step in range(1, OWNERS):
        rest_share(f, (f + step) % OWNERS).start()
    shares[f] = grads[f, 0:MODAL]
    shares_rest[f] = grads[f, MODAL:ROWS]
    for step in range(1, OWNERS):
        share_copy((f + step) % OWNERS, f).wait_recv()
    me = p // 2
    sums[me] = jnp.sum(shares[...], axis=0)

    def sum_copy(step, k, to):
        return remote(sums.at[k], sums.at[k], sum_s.at[step], sum_r.at[step], to, f)

    def sum_rest(step, k, to):
        return remote(sums_rest.at[k], sums_rest.at[k], sum2_s.at[step], sum2_r.at[step], to, f)

    for step in range(1, 8):
        sum_copy(step, me, (p + 2 * step) % 16).start()
    for step in range(1, OWNERS):
        rest_share((f + step) % OWNERS, f).wait_recv()
    sums_rest[me] = jnp.sum(shares_rest[...], axis=0)
    for step in range(1, 8):
        sum_rest(step, me, (p + 2 * step) % 16).start()
    for step in range(1, 8):
        sum_copy(step, (me + 8 - step) % 8, p).wait_recv()
    mine[0:MODAL] = jnp.sum(sums[...], axis=0)
    for step in range(1, 8):
        sum_rest(step, (me + 8 - step) % 8, p).wait_recv()
    mine[MODAL:ROWS] = jnp.sum(sums_rest[...], axis=0)
    end = remote(mine, other, end_s, end_r, partner, f)
    end.start()

    @pl.when(p < 15)
    def _():
        right.wait_send()

    @pl.when(p > 0)
    def _():
        left.wait_send()

    for step in range(1, OWNERS):
        to = (f + step) % OWNERS
        rest_copy(step, f, to).wait_send()
        modal_copy(step, f, to).wait_send()
        hand_copy(step, part).wait_send()
        share_copy(f, to).wait_send()
        rest_share(f, to).wait_send()

    def drain(o, _):
        copy1(o, e_all).wait_send()

        @pl.when(resident)
        def _():
            for j in range(1, 4):
                @pl.when(n + j < 4)
                def _():
                    copy3(o, j).wait_send()
            copy4(o).wait_send()

        @pl.when(jnp.logical_not(resident))
        def _():
            copy2(o).wait_send()
        copy5(o, whole).wait_send()
        for q in range(3):
            out_copy(o, q).wait()
        return 0

    lax.fori_loop(0, OWNERS, drain, 0)
    for step in range(1, 8):
        to = (p + 2 * step) % 16
        sum_copy(step, me, to).wait_send()
        sum_rest(step, me, to).wait_send()
    end.wait_recv()
    result[...] = mine[...] + other[...]
    end.wait_send()


def shape(*dims, dtype=F32):
    return jax.ShapeDtypeStruct(dims, dtype)


def per_device(rows_in, cotangent, taps, residues, rates, skip, state_before, adjoint_after):
    def buf(*dims, dtype=F32):
        return pltpu.VMEM(dims, dtype)

    def sems(*dims):
        return pltpu.SemaphoreType.DMA(dims)

    vec = buf(32, STEPS, 8, LANES)
    small = buf(OWNERS, 2 * MODES, LANES)
    each = [sems(16), sems(16)]
    grad_rows, total = pl.pallas_call(
        kernel,
        out_shape=(shape(1, 128, 12288, dtype=BF16), shape(ROWS, LANES)),
        in_specs=[ANY, ANY] + [VMEM] * 6,
        out_specs=(ANY, VMEM),
        scratch_shapes=[
            buf(1, 128, 12288, dtype=BF16), buf(1, 128, 4096, dtype=BF16), buf(1, 128, 12288, dtype=BF16),
            buf(OWNERS, ROWS, LANES), buf(OWNERS, ROWS, LANES), buf(192, LANES), buf(256, LANES),
            buf(192, LANES), buf(256, LANES), buf(192, LANES, dtype=BF16), buf(256, LANES, dtype=BF16),
            buf(192, LANES, dtype=BF16), buf(256, LANES, dtype=BF16),
            buf(128, LANES), buf(32, 3, 18, 8, LANES), buf(32, 2, STEPS, 8, LANES), vec, vec, vec,
            vec, vec, small, small, small, small, buf(STEPS, WIDTH, 8, LANES),
            buf(STEPS, 8, LANES), buf(STEPS, 8, LANES), buf(3, 18, 8, LANES), buf(4, MODES, LANES),
            small, small, buf(3, OWNERS, 2 * MODES, LANES), small, small, small, small, small, small,
            buf(OWNERS, MODAL, LANES), buf(OWNERS, REST, LANES), buf(8, MODAL, LANES), buf(8, REST, LANES),
            buf(ROWS, LANES), buf(ROWS, LANES),
            sems(2), sems(3, 16), sems(2), sems(2), *each, *each, *each,
            *each, *each, sems(3, 16), sems(3, 16), *each, *each,
            *each, *each, sems(8), sems(8), sems(8), sems(8), sems(), sems(),
        ],
        compiler_params=pltpu.CompilerParams(
            collective_id=1, has_side_effects=True, vmem_limit_bytes=56 * 2**20
        ),
        cost_estimate=pl.CostEstimate(flops=10**8, bytes_accessed=8 * 2**20, transcendentals=10**5),
        name="hyena",
    )(rows_in, cotangent, taps, residues, rates, skip[None, :], state_before, adjoint_after)
    return (
        grad_rows,
        total[64:82].reshape(3, 768),
        jnp.concatenate([total[0:16], total[16:32]], axis=1),
        jnp.concatenate([total[32:48], total[48:64]], axis=1),
        total[82:84].reshape(256),
    )


def solution(mesh):
    in_specs = (
        P("fsdp", "ctx", None),
        P("fsdp", "ctx", None),
        P(None, "fsdp"),
        P(None, "fsdp"),
        P(None, "fsdp"),
        P("fsdp"),
        P("fsdp", None, None),
        P("fsdp", None, None),
    )
    out_specs = (
        P("fsdp", "ctx", None),
        P(None, "fsdp"),
        P(None, "fsdp"),
        P(None, "fsdp"),
        P("fsdp"),
    )
    return jax.shard_map(
        per_device, mesh=mesh, in_specs=in_specs, out_specs=out_specs, check_vma=False
    )
```

time: 965 us -> 98.4 us (0.10)
  the two profiles are of different devices: /device:TPU:1 before, /device:TPU:65 now
where the time goes in v2:
time: 98.4 us; the launch traced here: 98 us
  Pallas kernels  89.6 us (91%)
  local copies, waits for them, and re-layouts  7.15 us (7%)
    pallas_call x1, Pallas kernels, per_device(): pl.pallas_call(kernel, out_shape=(shape(1, 128, 12288, dtype=BF16), shape...  89.6 us
    unnamed x1, local copies, waits for them, and re-layouts  3.83 us

profile of v2, /device:TPU:65, one launch (start us, length us, event | category | flops | bytes accessed | tf_op | source)
XLA Modules:
  0.0 98.0 jit_solution(17733620794237212292)
XLA Ops:
  0.6 89.6 %hyena.1 = (bf16[1,128,12288]{2,1,0:T(8,128)(2,1)}, f32[88,128]{1,0:T(8,128)}) custom-call(bf16[1,128,12288]{2,1,0:T(8,128)(2,1)} %rows_hbm.1, bf16[1,128,4096]{2,1,0:T(8,128)(2,1)} %cot_hbm.1, f32[3,768]{1,0:T(4,128)} %taps.1, f32[16,256]{1,0:T(8,128)} %residues.1, f32[16,256]{1,0:T(8,128)} %rates.1, f32[1,256]{1,0:T(1,128)} %bitcast.3, ...), custom_call_target="tpu_custom_call" | custom-call | flops 100000000 | bytes 8388608 | tf_op jit(solution)/shard_map/hyena/pallas_call | solution.py:575
  90.3 1.2 %slice_bitcast_fusion = f32[256]{0:T(256)} fusion(f32[88,128]{1,0:T(8,128)} %get-tuple-element.8), kind=kLoop, calls=%fused_computation.2 | loop fusion | bytes 2048 | tf_op jit(solution)/shard_map/reshape | solution.py:606
  91.5 0.7 slice.18
  92.2 0.7 fusion
  93.0 0.6 reshape.16
  93.6 0.6 pad_maximum_fusion
  94.2 3.8 %copy.14 = bf16[1,128,12288]{2,1,0:T(8,128)(2,1)} copy(bf16[1,128,12288]{2,1,0:T(8,128)(2,1)} %get-tuple-element.20) | data formatting | bytes 6291456

commit v3 on v2

--- a/solution.py
+++ b/solution.py
@@ -124,7 +124,7 @@
 
 
 def main_pass(group, edge, gath, nxt, xs, X, F, U, G, C, ends, starts, e_all, e_prior, s_prior,
-              out, grads, hist, filt, back, GB, weights):
+              grads, hist, filt, back, GB, weights):
     sub = sublane()
     scale = 1.0 / math.sqrt(16 * 2048)
     whole = own_rows(group, 0, MODES)
@@ -192,32 +192,38 @@
     u, g = U[group], G[group]
     grads[skip_at] = row_sum(jnp.sum(u * g, axis=0)) * scale
     mixed = back[...] + skip * g
-    GB[0, 0:16] = C[group] * (filt[...] + skip * u)
-    GB[1, 0:16] = mixed * F[group, 1]
-    GB[2, 0:16] = mixed * F[group, 0]
+    GB[group, 0, 0:16] = C[group] * (filt[...] + skip * u)
+    GB[group, 1, 0:16] = mixed * F[group, 1]
+    GB[group, 2, 0:16] = mixed * F[group, 0]
     for q in range(3):
-        t = [spread(taps[q][k]) for k in range(3)]
         for k in range(2):
             row = jnp.where(edge, 0.0, follow[q][k])
-            GB[q, 16 + k] = jnp.where(sub == 7, spread(row), pltpu.roll(GB[q, k], 7, 0))
-        grad = GB[q, 0:16]
+            GB[group, q, 16 + k] = jnp.where(sub == 7, spread(row), pltpu.roll(GB[group, q, k], 7, 0))
+        grad = GB[group, q, 0:16]
         for k in range(3):
             terms = X[group, q, 2 - k : 18 - k] * grad
             grads[tap_place(q, group, k)] = row_sum(jnp.sum(terms, axis=0)) * scale
-        y = t[0] * grad + t[1] * GB[q, 1:17] + t[2] * GB[q, 2:18]
+
+
+def rows_pass(group, gath, xs, GB, out):
+    for q in range(3):
+        t = [spread(gath[tap_place(q, group, k)]) for k in range(3)]
+        y = t[0] * GB[group, q, 0:16] + t[1] * GB[group, q, 1:17] + t[2] * GB[group, q, 2:18]
         for i in range(STEPS):
             xs[pl.ds(i, 8, stride=STEPS), :] = y[i]
         out[0, :, lanes_of(q * 32 + group)] = xs[...].astype(BF16)
 
 
-def kernel(rows_hbm, cot_hbm, taps, residues, rates, skip, before, after, rows_out, result,
-           rows, cot, out, gath, grads, prev, nxt, tail_f, head_f, tail_b, head_b, prev_b, next_b,
+def kernel(rows_hbm, cot_hbm, taps, residues, rates, skip, before_hbm, after_hbm,
+           rows_out, result,
+           rows, cot, before, after, out, gath, grads, prev, nxt, tail_f, head_f, tail_b, head_b, prev_b, next_b,
            xs, X, F, U, G, C, ends, starts, e_all, s_all, e_prior, s_prior, hist, filt, back, GB, weights,
-           first, second, third, whole, last, agg, chip, begin, inner,
-           shares, shares_rest, sums, sums_rest, mine, other,
+           first, second, third, whole, last, agg, chip, begin, inner, span,
+           by_y, by_z, relay, rest_y, rest_z, rest_sum, modal_x, modal_across, rest_x, rest_across,
+           mine, other,
            in_sem, out_sem, halo_s, halo_r, rest_s, rest_r, modal_s, modal_r, hand_s, hand_r,
            s1, r1, s2, r2, s3, r3, s4, r4, s5, r5,
-           share_s, share_r, share2_s, share2_r, sum_s, sum_r, sum2_s, sum2_r, end_s, end_r):
+           ys, yr, zs, zr, rys, ryr, rzs, rzr, mxs, mxr, mas, mar, rxs, rxr, ras, rar, end_s, end_r):
     p = lax.axis_index("ctx")
     f = lax.axis_index("fsdp")
     c, h, x = p % 2, (p // 2) % 2, p // 4
@@ -227,15 +233,29 @@
     n = jnp.where(c == 1, x, 3 - x)
     sign = jnp.where(c == 1, 4, -4)
     edge = p == 15
+    y, z = f // 4, f % 4
+    z_peers = [y * 4 + (z + k) % 4 for k in range(1, 4)]
+    y_peers = [(y + k) % 4 * 4 + z for k in range(1, 4)]
+
+    def owner_at(k):
+        turn_z = (k // 4 + 1) % 4
+        turn_y = (k + k // 12) % 4
+        return (y + turn_y) % 4 * 4 + (z + turn_z) % 4
+
+    def local_at(k):
+        return owner_at((k + 15) % 16)
 
     load_rows = pltpu.make_async_copy(rows_hbm, rows, in_sem.at[0])
     load_cot = pltpu.make_async_copy(cot_hbm, cot, in_sem.at[1])
-    load_rows.start()
-    load_cot.start()
-    for step in range(1, OWNERS):
-        greet(p, (f + step) % OWNERS)
-    for step in range(1, 8):
-        greet((p + 2 * step) % 16, f)
+    load_before = pltpu.make_async_copy(before_hbm, before, in_sem.at[2])
+    load_after = pltpu.make_async_copy(after_hbm, after, in_sem.at[3])
+    for load in (load_rows, load_cot, load_before, load_after):
+        load.start()
+    for peer in z_peers + y_peers:
+        greet(p, peer)
+    for step in range(1, 4):
+        greet((p + 4 * step) % 16, f)
+    greet(across, f)
     greet(partner, f)
     greet((p + 15 + 2 * c) % 16, f)
 
@@ -252,8 +272,29 @@
     for o in range(OWNERS):
         grads[o, 84:88, :] = jnp.zeros((4, LANES), F32)
 
-    load_rows.wait()
-    load_cot.wait()
+    pl.semaphore_wait(pltpu.get_barrier_semaphore(), 12)
+
+    def rest_copy(k, owner, to):
+        block = gath.at[owner, pl.ds(MODAL, REST)]
+        return remote(block, block, rest_s.at[k], rest_r.at[owner], p, to)
+
+    part = pl.multiple_of(32 - 32 * c, 32)
+    part_other = pl.multiple_of(32 * c, 32)
+
+    def modal_copy(k, owner, to):
+        block = gath.at[owner, pl.ds(part, 32)]
+        return remote(block, block, modal_s.at[k], modal_r.at[owner], p, to)
+
+    def hand_copy(owner, rows_from):
+        block = gath.at[owner, pl.ds(rows_from, 32)]
+        return remote(block, block, hand_s.at[owner], hand_r.at[owner], partner, f)
+
+    for make in (rest_copy, modal_copy):
+        for k, peer in enumerate(z_peers + y_peers):
+            make(k, f, peer).start()
+
+    for load in (load_rows, load_cot, load_before, load_after):
+        load.wait()
 
     def edges(unit, _):
         end = rows[0, 112:128, lanes_of(unit)].astype(F32)
@@ -270,11 +311,10 @@
         head_f[pl.ds(224 + unit, 1), :] = start[1:2]
         return 0
 
-    lax.fori_loop(0, 96, edges, 0)
-    lax.fori_loop(0, 32, edges_cot, 0)
+    lax.fori_loop(0, 96, edges, 0, unroll=4)
+    lax.fori_loop(0, 32, edges_cot, 0, unroll=4)
     tail_b[...] = tail_f[...].astype(BF16)
     head_b[...] = head_f[...].astype(BF16)
-    pl.semaphore_wait(pltpu.get_barrier_semaphore(), 24)
 
     right = remote(tail_b, prev_b, halo_s.at[0], halo_r.at[0], p + 1, f)
     left = remote(head_b, next_b, halo_s.at[1], halo_r.at[1], p - 1, f)
@@ -287,25 +327,11 @@
     def _():
         left.start()
 
-    def rest_copy(step, owner, to):
-        block = gath.at[owner, pl.ds(MODAL, REST)]
-        return remote(block, block, rest_s.at[step], rest_r.at[step], p, to)
-
-    part = pl.multiple_of(32 - 32 * c, 32)
-    part_other = pl.multiple_of(32 * c, 32)
-
-    def modal_copy(step, owner, to):
-        block = gath.at[owner, pl.ds(part, 32)]
-        return remote(block, block, modal_s.at[step], modal_r.at[step], p, to)
-
-    def hand_copy(step, rows_from):
-        block = gath.at[(f + step) % OWNERS, pl.ds(rows_from, 32)]
-        return remote(block, block, hand_s.at[step], hand_r.at[step], partner, f)
-
-    for step in range(1, OWNERS):
-        rest_copy(step, f, (f + OWNERS - step) % OWNERS).start()
-    for step in range(1, OWNERS):
-        modal_copy(step, f, (f + OWNERS - step) % OWNERS).start()
+    for make in (rest_copy, modal_copy):
+        for k, owner in enumerate(z_peers):
+            make(0, owner, f).wait_recv()
+            for j, peer in enumerate(y_peers):
+                make(6 + 3 * k + j, owner, peer).start()
 
     @pl.when(p > 0)
     def _():
@@ -325,15 +351,18 @@
     def _():
         nxt[...] = jnp.zeros_like(nxt)
 
-    for step in range(1, OWNERS):
-        rest_copy(step, (f + step) % OWNERS, f).wait_recv()
-
-    def hand_on(step):
-        modal_copy(step, (f + step) % OWNERS, f).wait_recv()
-        hand_copy(step, part).start()
-
-    for step in range(1, 1 + AHEAD):
-        hand_on(step)
+    for k in range(4):
+        for peer in y_peers:
+            rest_copy(0, peer // 4 * 4 + (z + k) % 4, f).wait_recv()
+
+    def hand_on(owner):
+        @pl.when(owner // 4 != y)
+        def _():
+            modal_copy(0, owner, f).wait_recv()
+        hand_copy(owner, part).start()
+
+    for k in range(1, 1 + AHEAD):
+        hand_on(local_at(k))
 
     def copy1(o, ref):
         return remote(ref.at[o], first.at[o], s1.at[o], r1.at[o], partner, f)
@@ -351,10 +380,14 @@
         return remote(ref.at[o], last.at[o], s5.at[o], r5.at[o], partner, f)
 
     def decay(o, power):
-        return jnp.exp(gath[o, 32:64, :] * (-128.0 * power))
+        value = span[o]
+        for _ in range(power // 2):
+            value = value * value
+        return value
 
     def stage1(o):
         copy1(o, e_all).wait_recv()
+        span[o] = jnp.exp(gath[o, 32:64, :] * -128.0)
         own = jnp.where(c == 1, e_all[o], s_all[o])
         agg[o] = own + decay(o, 1) * first[o]
 
@@ -387,12 +420,12 @@
             for b in range(2):
                 cols = lanes_of(2 * o + b)
                 begin[o, 16 * b : 16 * (b + 1), :] = jnp.where(c == 1, before[0, :, cols], after[0, :, cols])
-            span = decay(o, 4)
+            four = decay(o, 4)
             for j in range(3, 0, -1):
                 @pl.when(n >= j)
                 def _():
                     copy3(o, j).wait_recv()
-                    begin[o] = third[j - 1, o] + span * begin[o]
+                    begin[o] = third[j - 1, o] + four * begin[o]
             copy4(o).start()
             inner[o] = decay(o, 2) * begin[o] + second[o]
             copy5(o, inner).start()
@@ -416,29 +449,41 @@
         def _():
             e_prior[o] = last[o]
 
-    def share_copy(source, to):
-        return remote(grads.at[to, pl.ds(0, MODAL)], shares.at[source],
-                      share_s.at[to], share_r.at[source], p, to)
-
-    def rest_share(source, to):
-        return remote(grads.at[to, pl.ds(MODAL, REST)], shares_rest.at[source],
-                      share2_s.at[to], share2_r.at[source], p, to)
-
-    def out_copy(o, q):
-        block = (slice(None), slice(None), lanes_of(q * 32 + 2 * o, 2))
-        return pltpu.make_async_copy(out.at[block], rows_out.at[block], out_sem.at[q, o])
+    def share_copy(owner, source, to):
+        return remote(grads.at[owner, pl.ds(0, MODAL)], by_y.at[owner % 4, source],
+                      ys.at[owner], yr.at[owner % 4, source], p, to)
+
+    def relay_copy(to_z, from_z):
+        return remote(relay.at[to_z], by_z.at[from_z], zs.at[to_z], zr.at[from_z], p, y * 4 + to_z)
+
+    def gather_y(owner):
+        for k in range(1, 4):
+            share_copy(owner, (y + k) % 4, f).wait_recv()
+        by_y[owner % 4, y] = grads[owner, 0:MODAL]
+        return jnp.sum(by_y[owner % 4], axis=0)
+
+    def relay_one(to_z):
+        relay[to_z] = gather_y(y * 4 + to_z)
+        relay_copy(to_z, z).start()
+
+    def write_rows(begin_group, end_group):
+        def one(group, _):
+            rows_pass(group, gath, xs, GB, out)
+            return 0
+
+        lax.fori_loop(begin_group, end_group, one, 0)
 
     def turn(t, _):
         @pl.when(t < OWNERS)
         def _():
             @pl.when(t + AHEAD + 1 < OWNERS)
             def _():
-                hand_on(t + AHEAD + 1)
+                hand_on(local_at(t + AHEAD + 1))
+            o = local_at(t)
 
             @pl.when(t > 0)
             def _():
-                hand_copy(t, part_other).wait_recv()
-            o = (f + t) % OWNERS
+                hand_copy(o, part_other).wait_recv()
 
             def one(j, _):
                 local_pass(2 * o + j, rows, cot, gath, prev, xs, X, F, U, G, C, ends, starts,
@@ -459,57 +504,88 @@
                            (stage1, STAGE1)):
             @pl.when(jnp.logical_and(t >= lag, t < lag + OWNERS))
             def _():
-                stage((f + t - lag) % OWNERS)
+                stage(local_at(t - lag))
 
         @pl.when(t >= MAIN)
         def _():
-            o = (f + t - MAIN + 1) % OWNERS
+            o = owner_at(t - MAIN)
 
             def one(j, _):
                 main_pass(2 * o + j, edge, gath, nxt, xs, X, F, U, G, C, ends, starts, e_all,
-                          e_prior, s_prior, out, grads, hist, filt, back, GB, weights)
+                          e_prior, s_prior, grads, hist, filt, back, GB, weights)
                 return 0
 
             lax.fori_loop(0, 2, one, 0)
-            for q in range(3):
-                out_copy(o, q).start()
-
-            @pl.when(t < TURNS - 1)
+
+            @pl.when(o // 4 != y)
             def _():
-                share_copy(f, o).start()
+                share_copy(o, y, o // 4 * 4 + z).start()
+
+        for k in range(1, 4):
+            @pl.when(t == MAIN + 4 * k + 1)
+            def _():
+                relay_one((z + k) % 4)
 
         return 0
 
     lax.fori_loop(0, TURNS, turn, 0)
 
-    for step in range(1, OWNERS):
-        rest_share(f, (f + step) % OWNERS).start()
-    shares[f] = grads[f, 0:MODAL]
-    shares_rest[f] = grads[f, MODAL:ROWS]
-    for step in range(1, OWNERS):
-        share_copy((f + step) % OWNERS, f).wait_recv()
-    me = p // 2
-    sums[me] = jnp.sum(shares[...], axis=0)
-
-    def sum_copy(step, k, to):
-        return remote(sums.at[k], sums.at[k], sum_s.at[step], sum_r.at[step], to, f)
-
-    def sum_rest(step, k, to):
-        return remote(sums_rest.at[k], sums_rest.at[k], sum2_s.at[step], sum2_r.at[step], to, f)
-
-    for step in range(1, 8):
-        sum_copy(step, me, (p + 2 * step) % 16).start()
-    for step in range(1, OWNERS):
-        rest_share((f + step) % OWNERS, f).wait_recv()
-    sums_rest[me] = jnp.sum(shares_rest[...], axis=0)
-    for step in range(1, 8):
-        sum_rest(step, me, (p + 2 * step) % 16).start()
-    for step in range(1, 8):
-        sum_copy(step, (me + 8 - step) % 8, p).wait_recv()
-    mine[0:MODAL] = jnp.sum(sums[...], axis=0)
-    for step in range(1, 8):
-        sum_rest(step, (me + 8 - step) % 8, p).wait_recv()
-    mine[MODAL:ROWS] = jnp.sum(sums_rest[...], axis=0)
+    def rest_to_y(to_y, from_y):
+        return remote(grads.at[pl.ds(4 * to_y, 4), pl.ds(MODAL, REST)], rest_y.at[from_y],
+                      rys.at[to_y], ryr.at[from_y], p, to_y * 4 + z)
+
+    def rest_to_z(to_z, from_z):
+        return remote(rest_sum.at[to_z], rest_z.at[from_z], rzs.at[to_z], rzr.at[from_z], p, y * 4 + to_z)
+
+    def over_x(ref, send, recv, k, slot):
+        return remote(ref.at[slot], ref.at[slot], send.at[k], recv.at[slot], (p + 4 * k) % 16, f)
+
+    def over_across(ref, send, recv, slot):
+        return remote(ref.at[slot], ref.at[slot], send, recv, across, f)
+
+    for k in range(1, 4):
+        rest_to_y((y + k) % 4, y).start()
+    write_rows(0, 10)
+    total = gather_y(f)
+    for k in range(1, 4):
+        relay_copy(z, (z + k) % 4).wait_recv()
+    by_z[z] = total
+    modal_x[x] = jnp.sum(by_z[...], axis=0)
+    for k in range(1, 4):
+        over_x(modal_x, mxs, mxr, k, x).start()
+
+    rest_y[y] = grads[pl.ds(4 * y, 4), MODAL:ROWS, :]
+    for k in range(1, 4):
+        rest_to_y(y, (y + k) % 4).wait_recv()
+    rest_sum[...] = jnp.sum(rest_y[...], axis=0)
+    for k in range(1, 4):
+        rest_to_z((z + k) % 4, z).start()
+    write_rows(10, 22)
+
+    for k in range(1, 4):
+        over_x(modal_x, mxs, mxr, k, (x + k) % 4).wait_recv()
+    modal_across[h] = jnp.sum(modal_x[...], axis=0)
+    over_across(modal_across, mas, mar, h).start()
+
+    rest_z[z] = rest_sum[z]
+    for k in range(1, 4):
+        rest_to_z(z, (z + k) % 4).wait_recv()
+    rest_x[x] = jnp.sum(rest_z[...], axis=0)
+    for k in range(1, 4):
+        over_x(rest_x, rxs, rxr, k, x).start()
+    write_rows(22, 32)
+    store = pltpu.make_async_copy(out, rows_out, out_sem)
+    store.start()
+
+    over_across(modal_across, mas, mar, 1 - h).wait_recv()
+    mine[0:MODAL] = modal_across[0] + modal_across[1]
+
+    for k in range(1, 4):
+        over_x(rest_x, rxs, rxr, k, (x + k) % 4).wait_recv()
+    rest_across[h] = jnp.sum(rest_x[...], axis=0)
+    over_across(rest_across, ras, rar, h).start()
+    over_across(rest_across, ras, rar, 1 - h).wait_recv()
+    mine[MODAL:ROWS] = rest_across[0] + rest_across[1]
     end = remote(mine, other, end_s, end_r, partner, f)
     end.start()
 
@@ -521,13 +597,17 @@
     def _():
         left.wait_send()
 
-    for step in range(1, OWNERS):
-        to = (f + step) % OWNERS
-        rest_copy(step, f, to).wait_send()
-        modal_copy(step, f, to).wait_send()
-        hand_copy(step, part).wait_send()
-        share_copy(f, to).wait_send()
-        rest_share(f, to).wait_send()
+    for k in range(15):
+        rest_copy(k, f, f).wait_send()
+        modal_copy(k, f, f).wait_send()
+    for k in range(1, 4):
+        relay_copy((z + k) % 4, z).wait_send()
+        rest_to_y((y + k) % 4, y).wait_send()
+        rest_to_z((z + k) % 4, z).wait_send()
+        over_x(modal_x, mxs, mxr, k, x).wait_send()
+        over_x(rest_x, rxs, rxr, k, x).wait_send()
+    over_across(modal_across, mas, mar, h).wait_send()
+    over_across(rest_across, ras, rar, h).wait_send()
 
     def drain(o, _):
         copy1(o, e_all).wait_send()
@@ -544,20 +624,46 @@
         def _():
             copy2(o).wait_send()
         copy5(o, whole).wait_send()
-        for q in range(3):
-            out_copy(o, q).wait()
+
+        @pl.when(o != f)
+        def _():
+            hand_copy(o, part).wait_send()
+
+        @pl.when(o // 4 != y)
+        def _():
+            share_copy(o, y, f).wait_send()
         return 0
 
     lax.fori_loop(0, OWNERS, drain, 0)
-    for step in range(1, 8):
-        to = (p + 2 * step) % 16
-        sum_copy(step, me, to).wait_send()
-        sum_rest(step, me, to).wait_send()
+    store.wait()
     end.wait_recv()
     result[...] = mine[...] + other[...]
     end.wait_send()
 
 
+def finish(rows_in, mine, rows_out, taps_out, res_out, rate_out, skip_out, held, load_sem, store_sem):
+    def piece(k):
+        return slice(None), slice(16 * k, 16 * (k + 1))
+
+    loads = [pltpu.make_async_copy(rows_in.at[piece(k)], held.at[piece(k)], load_sem.at[k]) for k in range(8)]
+    stores = [pltpu.make_async_copy(held.at[piece(k)], rows_out.at[piece(k)], store_sem.at[k]) for k in range(8)]
+    for load in loads:
+        load.start()
+    for b in range(2):
+        cols = slice(LANES * b, LANES * (b + 1))
+        res_out[:, cols] = mine[16 * b : 16 * (b + 1), :]
+        rate_out[:, cols] = mine[32 + 16 * b : 48 + 16 * b, :]
+        skip_out[:, cols] = mine[82 + b : 83 + b, :]
+    for j in range(3):
+        for b in range(6):
+            row = MODAL + 6 * j + b
+            taps_out[j : j + 1, LANES * b : LANES * (b + 1)] = mine[row : row + 1, :]
+    for load, store in zip(loads, stores):
+        load.wait()
+        store.start()
+    for store in stores:
+        store.wait()
+
 def shape(*dims, dtype=F32):
     return jax.ShapeDtypeStruct(dims, dtype)
 
@@ -572,25 +678,30 @@
     vec = buf(32, STEPS, 8, LANES)
     small = buf(OWNERS, 2 * MODES, LANES)
     each = [sems(16), sems(16)]
-    grad_rows, total = pl.pallas_call(
+    four = [sems(4), sems(4)]
+    one = [sems(), sems()]
+    rows_sum, total = pl.pallas_call(
         kernel,
         out_shape=(shape(1, 128, 12288, dtype=BF16), shape(ROWS, LANES)),
-        in_specs=[ANY, ANY] + [VMEM] * 6,
+        in_specs=[ANY, ANY] + [VMEM] * 4 + [ANY, ANY],
         out_specs=(ANY, VMEM),
         scratch_shapes=[
-            buf(1, 128, 12288, dtype=BF16), buf(1, 128, 4096, dtype=BF16), buf(1, 128, 12288, dtype=BF16),
+            buf(1, 128, 12288, dtype=BF16), buf(1, 128, 4096, dtype=BF16), buf(1, MODES, 4096), buf(1, MODES, 4096),
+            buf(1, 128, 12288, dtype=BF16),
             buf(OWNERS, ROWS, LANES), buf(OWNERS, ROWS, LANES), buf(192, LANES), buf(256, LANES),
             buf(192, LANES), buf(256, LANES), buf(192, LANES, dtype=BF16), buf(256, LANES, dtype=BF16),
             buf(192, LANES, dtype=BF16), buf(256, LANES, dtype=BF16),
             buf(128, LANES), buf(32, 3, 18, 8, LANES), buf(32, 2, STEPS, 8, LANES), vec, vec, vec,
             vec, vec, small, small, small, small, buf(STEPS, WIDTH, 8, LANES),
-            buf(STEPS, 8, LANES), buf(STEPS, 8, LANES), buf(3, 18, 8, LANES), buf(4, MODES, LANES),
-            small, small, buf(3, OWNERS, 2 * MODES, LANES), small, small, small, small, small, small,
-            buf(OWNERS, MODAL, LANES), buf(OWNERS, REST, LANES), buf(8, MODAL, LANES), buf(8, REST, LANES),
+            buf(STEPS, 8, LANES), buf(STEPS, 8, LANES), buf(32, 3, 18, 8, LANES), buf(4, MODES, LANES),
+            small, small, buf(3, OWNERS, 2 * MODES, LANES), small, small, small, small, small, small, small,
+            buf(4, 4, MODAL, LANES), buf(4, MODAL, LANES), buf(4, MODAL, LANES),
+            buf(4, 4, REST, LANES), buf(4, REST, LANES), buf(4, REST, LANES),
+            buf(4, MODAL, LANES), buf(2, MODAL, LANES), buf(4, REST, LANES), buf(2, REST, LANES),
             buf(ROWS, LANES), buf(ROWS, LANES),
-            sems(2), sems(3, 16), sems(2), sems(2), *each, *each, *each,
+            sems(4), sems(), sems(2), sems(2), *each, *each, *each,
             *each, *each, sems(3, 16), sems(3, 16), *each, *each,
-            *each, *each, sems(8), sems(8), sems(8), sems(8), sems(), sems(),
+            sems(16), sems(4, 4), *four, *four, *four, *four, *one, *four, *one, *one,
         ],
         compiler_params=pltpu.CompilerParams(
             collective_id=1, has_side_effects=True, vmem_limit_bytes=56 * 2**20
@@ -598,12 +709,22 @@
         cost_estimate=pl.CostEstimate(flops=10**8, bytes_accessed=8 * 2**20, transcendentals=10**5),
         name="hyena",
     )(rows_in, cotangent, taps, residues, rates, skip[None, :], state_before, adjoint_after)
+    grad_rows, taps_sum, res_sum, rate_sum, skip_sum = pl.pallas_call(
+        finish,
+        out_shape=(shape(1, 128, 12288, dtype=BF16), shape(3, 768), shape(16, 256), shape(16, 256),
+                   shape(1, 256)),
+        in_specs=[ANY, VMEM],
+        out_specs=(ANY,) + (VMEM,) * 4,
+        scratch_shapes=[buf(1, 128, 12288, dtype=BF16), sems(8), sems(8)],
+        compiler_params=pltpu.CompilerParams(vmem_limit_bytes=56 * 2**20),
+        name="finish",
+    )(rows_sum, total)
     return (
         grad_rows,
-        total[64:82].reshape(3, 768),
-        jnp.concatenate([total[0:16], total[16:32]], axis=1),
-        jnp.concatenate([total[32:48], total[48:64]], axis=1),
-        total[82:84].reshape(256),
+        taps_sum,
+        res_sum,
+        rate_sum,
+        skip_sum.reshape(256),
     )
 
 

time: 98.4 us -> 90.3 us (0.918)
  the two profiles are of different devices: /device:TPU:65 before, /device:TPU:1 now
where the time goes in v3:
time: 90.3 us; the launch traced here: 89.4 us
  Pallas kernels  88.7 us (98%)
    pallas_call x1, Pallas kernels, per_device(): pl.pallas_call(kernel, out_shape=(shape(1, 128, 12288, dtype=BF16), shape...  84.5 us
    pallas_call x1, Pallas kernels, per_device(): pl.pallas_call(finish, out_shape=(shape(1, 128, 12288, dtype=BF16), shape...  4.19 us

profile of v3, /device:TPU:1, one launch (start us, length us, event | category | flops | bytes accessed | tf_op | source)
XLA Modules:
  0.0 89.4 jit_solution(5755851043642569651)
XLA Ops:
  0.6 84.5 %hyena.1 = (bf16[1,128,12288]{2,1,0:T(8,128)(2,1)}, f32[88,128]{1,0:T(8,128)}) custom-call(bf16[1,128,12288]{2,1,0:T(8,128)(2,1)} %rows_hbm.1, bf16[1,128,4096]{2,1,0:T(8,128)(2,1)} %cot_hbm.1, f32[3,768]{1,0:T(4,128)} %taps.1, f32[16,256]{1,0:T(8,128)} %residues.1, f32[16,256]{1,0:T(8,128)} %rates.1, f32[1,256]{1,0:T(1,128)} %bitcast.2, ...), custom_call_target="tpu_custom_call" | custom-call | flops 100000000 | bytes 8388608 | tf_op jit(solution)/shard_map/hyena/pallas_call | solution.py:683
  85.2 4.2 %finish.1 = (bf16[1,128,12288]{2,1,0:T(8,128)(2,1)}, f32[3,768]{1,0:T(4,128)}, f32[16,256]{1,0:T(8,128)}, f32[16,256]{1,0:T(8,128)}, f32[1,256]{1,0:T(1,128)}) custom-call(bf16[1,128,12288]{2,1,0:T(8,128)(2,1)} %get-tuple-element.12.rows_in, f32[88,128]{1,0:T(8,128)} %get-tuple-element.13.mine), custom_call_target="tpu_custom_call" | custom-call | tf_op jit(solution)/shard_map/finish/pallas_call | solution.py:712

commit v4 on v3

--- a/solution.py
+++ b/solution.py
@@ -19,7 +19,7 @@
 REST = ROWS - MODAL
 WIDTH = 8
 AHEAD = 4
-STAGE1, STAGE2, STAGE3, STAGE4, STAGE5 = 1, 7, 10, 16, 17
+STAGE1, STAGE2, STAGE3, STAGE4, STAGE5 = 1, 5, 8, 12, 13
 MAIN = STAGE5 + 1
 TURNS = MAIN + OWNERS
 VMEM = pl.BlockSpec(memory_space=pltpu.VMEM)

time: 90.3 us -> 89 us (0.986)
  no operation moved by 1% of the time
where the time goes in v4:
time: 89 us; the launch traced here: 88.8 us
  Pallas kernels  88.2 us (99%)
    pallas_call x1, Pallas kernels, per_device(): pl.pallas_call(kernel, out_shape=(shape(1, 128, 12288, dtype=BF16), shape...  84 us
    pallas_call x1, Pallas kernels, per_device(): pl.pallas_call(finish, out_shape=(shape(1, 128, 12288, dtype=BF16), shape...  4.19 us

profile of v4, /device:TPU:1, one launch (start us, length us, event | category | flops | bytes accessed | tf_op | source)
XLA Modules:
  0.0 88.8 jit_solution(14867064560266110225)
XLA Ops:
  0.6 84.0 %hyena.1 = (bf16[1,128,12288]{2,1,0:T(8,128)(2,1)}, f32[88,128]{1,0:T(8,128)}) custom-call(bf16[1,128,12288]{2,1,0:T(8,128)(2,1)} %rows_hbm.1, bf16[1,128,4096]{2,1,0:T(8,128)(2,1)} %cot_hbm.1, f32[3,768]{1,0:T(4,128)} %taps.1, f32[16,256]{1,0:T(8,128)} %residues.1, f32[16,256]{1,0:T(8,128)} %rates.1, f32[1,256]{1,0:T(1,128)} %bitcast.2, ...), custom_call_target="tpu_custom_call" | custom-call | flops 100000000 | bytes 8388608 | tf_op jit(solution)/shard_map/hyena/pallas_call | solution.py:683
  84.6 4.2 %finish.1 = (bf16[1,128,12288]{2,1,0:T(8,128)(2,1)}, f32[3,768]{1,0:T(4,128)}, f32[16,256]{1,0:T(8,128)}, f32[16,256]{1,0:T(8,128)}, f32[1,256]{1,0:T(1,128)}) custom-call(bf16[1,128,12288]{2,1,0:T(8,128)(2,1)} %get-tuple-element.12.rows_in, f32[88,128]{1,0:T(8,128)} %get-tuple-element.13.mine), custom_call_target="tpu_custom_call" | custom-call | tf_op jit(solution)/shard_map/finish/pallas_call | solution.py:712

commit v5 on v4

--- a/solution.py
+++ b/solution.py
@@ -215,13 +215,13 @@
 
 
 def kernel(rows_hbm, cot_hbm, taps, residues, rates, skip, before_hbm, after_hbm,
-           rows_out, result,
-           rows, cot, before, after, out, gath, grads, prev, nxt, tail_f, head_f, tail_b, head_b, prev_b, next_b,
+           out, result,
+           rows, cot, before, after, gath, grads, prev, nxt, tail_f, head_f, tail_b, head_b, prev_b, next_b,
            xs, X, F, U, G, C, ends, starts, e_all, s_all, e_prior, s_prior, hist, filt, back, GB, weights,
            first, second, third, whole, last, agg, chip, begin, inner, span,
            by_y, by_z, relay, rest_y, rest_z, rest_sum, modal_x, modal_across, rest_x, rest_across,
            mine, other,
-           in_sem, out_sem, halo_s, halo_r, rest_s, rest_r, modal_s, modal_r, hand_s, hand_r,
+           in_sem, halo_s, halo_r, rest_s, rest_r, modal_s, modal_r, hand_s, hand_r,
            s1, r1, s2, r2, s3, r3, s4, r4, s5, r5,
            ys, yr, zs, zr, rys, ryr, rzs, rzr, mxs, mxr, mas, mar, rxs, rxr, ras, rar, end_s, end_r):
     p = lax.axis_index("ctx")
@@ -574,8 +574,6 @@
     for k in range(1, 4):
         over_x(rest_x, rxs, rxr, k, x).start()
     write_rows(22, 32)
-    store = pltpu.make_async_copy(out, rows_out, out_sem)
-    store.start()
 
     over_across(modal_across, mas, mar, 1 - h).wait_recv()
     mine[0:MODAL] = modal_across[0] + modal_across[1]
@@ -635,20 +633,18 @@
         return 0
 
     lax.fori_loop(0, OWNERS, drain, 0)
-    store.wait()
     end.wait_recv()
     result[...] = mine[...] + other[...]
     end.wait_send()
 
 
-def finish(rows_in, mine, rows_out, taps_out, res_out, rate_out, skip_out, held, load_sem, store_sem):
+def finish(rows_in, mine, rows_out, taps_out, res_out, rate_out, skip_out, store_sem):
     def piece(k):
         return slice(None), slice(16 * k, 16 * (k + 1))
 
-    loads = [pltpu.make_async_copy(rows_in.at[piece(k)], held.at[piece(k)], load_sem.at[k]) for k in range(8)]
-    stores = [pltpu.make_async_copy(held.at[piece(k)], rows_out.at[piece(k)], store_sem.at[k]) for k in range(8)]
-    for load in loads:
-        load.start()
+    stores = [pltpu.make_async_copy(rows_in.at[piece(k)], rows_out.at[piece(k)], store_sem.at[k]) for k in range(8)]
+    for store in stores:
+        store.start()
     for b in range(2):
         cols = slice(LANES * b, LANES * (b + 1))
         res_out[:, cols] = mine[16 * b : 16 * (b + 1), :]
@@ -658,9 +654,6 @@
         for b in range(6):
             row = MODAL + 6 * j + b
             taps_out[j : j + 1, LANES * b : LANES * (b + 1)] = mine[row : row + 1, :]
-    for load, store in zip(loads, stores):
-        load.wait()
-        store.start()
     for store in stores:
         store.wait()
 
@@ -682,12 +675,11 @@
     one = [sems(), sems()]
     rows_sum, total = pl.pallas_call(
         kernel,
-        out_shape=(shape(1, 128, 12288, dtype=BF16), shape(ROWS, LANES)),
+        out_shape=(pltpu.VMEM((1, 128, 12288), BF16), pltpu.VMEM((ROWS, LANES), F32)),
         in_specs=[ANY, ANY] + [VMEM] * 4 + [ANY, ANY],
-        out_specs=(ANY, VMEM),
+        out_specs=(VMEM, VMEM),
         scratch_shapes=[
             buf(1, 128, 12288, dtype=BF16), buf(1, 128, 4096, dtype=BF16), buf(1, MODES, 4096), buf(1, MODES, 4096),
-            buf(1, 128, 12288, dtype=BF16),
             buf(OWNERS, ROWS, LANES), buf(OWNERS, ROWS, LANES), buf(192, LANES), buf(256, LANES),
             buf(192, LANES), buf(256, LANES), buf(192, LANES, dtype=BF16), buf(256, LANES, dtype=BF16),
             buf(192, LANES, dtype=BF16), buf(256, LANES, dtype=BF16),
@@ -699,7 +691,7 @@
             buf(4, 4, REST, LANES), buf(4, REST, LANES), buf(4, REST, LANES),
             buf(4, MODAL, LANES), buf(2, MODAL, LANES), buf(4, REST, LANES), buf(2, REST, LANES),
             buf(ROWS, LANES), buf(ROWS, LANES),
-            sems(4), sems(), sems(2), sems(2), *each, *each, *each,
+            sems(4), sems(2), sems(2), *each, *each, *each,
             *each, *each, sems(3, 16), sems(3, 16), *each, *each,
             sems(16), sems(4, 4), *four, *four, *four, *four, *one, *four, *one, *one,
         ],
@@ -713,10 +705,10 @@
         finish,
         out_shape=(shape(1, 128, 12288, dtype=BF16), shape(3, 768), shape(16, 256), shape(16, 256),
                    shape(1, 256)),
-        in_specs=[ANY, VMEM],
+        in_specs=[VMEM, VMEM],
         out_specs=(ANY,) + (VMEM,) * 4,
-        scratch_shapes=[buf(1, 128, 12288, dtype=BF16), sems(8), sems(8)],
-        compiler_params=pltpu.CompilerParams(vmem_limit_bytes=56 * 2**20),
+        scratch_shapes=[sems(8)],
+        compiler_params=pltpu.CompilerParams(vmem_limit_bytes=16 * 2**20),
         name="finish",
     )(rows_sum, total)
     return (

time: 89 us -> 86.5 us (0.972)
  Pallas kernels: 88.2 us -> 85.7 us
    pallas_call x1, Pallas kernels: 4.19 us -> 2.34 us  [per_device(): pl.pallas_call(finish, out_shape=(shape(1, 128, 12288, dtype=BF16), shape...]
where the time goes in v5:
time: 86.5 us; the launch traced here: 86.3 us
  Pallas kernels  85.7 us (99%)
    pallas_call x1, Pallas kernels, per_device(): pl.pallas_call(kernel, out_shape=(pltpu.VMEM((1, 128, 12288), BF16), pltp...  83.4 us
    pallas_call x1, Pallas kernels, per_device(): pl.pallas_call(finish, out_shape=(shape(1, 128, 12288, dtype=BF16), shape...  2.34 us

profile of v5, /device:TPU:1, one launch (start us, length us, event | category | flops | bytes accessed | tf_op | source)
XLA Modules:
  0.0 86.3 jit_solution(1236289216112664960)
XLA Ops:
  0.6 83.4 %hyena.1 = (bf16[1,128,12288]{2,1,0:T(8,128)(2,1)S(1)}, f32[88,128]{1,0:T(8,128)S(1)}) custom-call(bf16[1,128,12288]{2,1,0:T(8,128)(2,1)} %rows_hbm.1, bf16[1,128,4096]{2,1,0:T(8,128)(2,1)} %cot_hbm.1, f32[3,768]{1,0:T(4,128)} %taps.1, f32[16,256]{1,0:T(8,128)} %residues.1, f32[16,256]{1,0:T(8,128)} %rates.1, f32[1,256]{1,0:T(1,128)} %bitcast.2, ...), custom_call_target="tpu_custom_call" | custom-call | flops 100000000 | bytes 8388608 | tf_op jit(solution)/shard_map/hyena/pallas_call | solution.py:676
  84.0 2.3 %finish.1 = (bf16[1,128,12288]{2,1,0:T(8,128)(2,1)}, f32[3,768]{1,0:T(4,128)}, f32[16,256]{1,0:T(8,128)}, f32[16,256]{1,0:T(8,128)}, f32[1,256]{1,0:T(1,128)}) custom-call(bf16[1,128,12288]{2,1,0:T(8,128)(2,1)S(1)} %get-tuple-element.12.rows_in, f32[88,128]{1,0:T(8,128)S(1)} %get-tuple-element.13.mine), custom_call_target="tpu_custom_call" | custom-call | tf_op jit(solution)/shard_map/finish/pallas_call | solution.py:704

commit v6 on v5

--- a/solution.py
+++ b/solution.py
@@ -468,7 +468,7 @@
 
     def write_rows(begin_group, end_group):
         def one(group, _):
-            rows_pass(group, gath, xs, GB, out)
+            rows_pass(group, gath, xs.at[0], GB, out)
             return 0
 
         lax.fori_loop(begin_group, end_group, one, 0)
@@ -485,12 +485,9 @@
             def _():
                 hand_copy(o, part_other).wait_recv()
 
-            def one(j, _):
-                local_pass(2 * o + j, rows, cot, gath, prev, xs, X, F, U, G, C, ends, starts,
-                           e_all, s_all, weights)
-                return 0
-
-            lax.fori_loop(0, 2, one, 0)
+            for j in range(2):
+                local_pass(2 * o + j, rows, cot, gath, prev, xs.at[j], X, F, U, G, C, ends, starts,
+                           e_all, s_all, weights.at[j])
 
             @pl.when(c == 0)
             def _():
@@ -510,12 +507,9 @@
         def _():
             o = owner_at(t - MAIN)
 
-            def one(j, _):
-                main_pass(2 * o + j, edge, gath, nxt, xs, X, F, U, G, C, ends, starts, e_all,
-                          e_prior, s_prior, grads, hist, filt, back, GB, weights)
-                return 0
-
-            lax.fori_loop(0, 2, one, 0)
+            for j in range(2):
+                main_pass(2 * o + j, edge, gath, nxt, xs.at[j], X, F, U, G, C, ends, starts, e_all,
+                          e_prior, s_prior, grads, hist, filt, back, GB, weights.at[j])
 
             @pl.when(o // 4 != y)
             def _():
@@ -683,9 +677,9 @@
             buf(OWNERS, ROWS, LANES), buf(OWNERS, ROWS, LANES), buf(192, LANES), buf(256, LANES),
             buf(192, LANES), buf(256, LANES), buf(192, LANES, dtype=BF16), buf(256, LANES, dtype=BF16),
             buf(192, LANES, dtype=BF16), buf(256, LANES, dtype=BF16),
-            buf(128, LANES), buf(32, 3, 18, 8, LANES), buf(32, 2, STEPS, 8, LANES), vec, vec, vec,
+            buf(2, 128, LANES), buf(32, 3, 18, 8, LANES), buf(32, 2, STEPS, 8, LANES), vec, vec, vec,
             vec, vec, small, small, small, small, buf(STEPS, WIDTH, 8, LANES),
-            buf(STEPS, 8, LANES), buf(STEPS, 8, LANES), buf(32, 3, 18, 8, LANES), buf(4, MODES, LANES),
+            buf(STEPS, 8, LANES), buf(STEPS, 8, LANES), buf(32, 3, 18, 8, LANES), buf(2, 4, MODES, LANES),
             small, small, buf(3, OWNERS, 2 * MODES, LANES), small, small, small, small, small, small, small,
             buf(4, 4, MODAL, LANES), buf(4, MODAL, LANES), buf(4, MODAL, LANES),
             buf(4, 4, REST, LANES), buf(4, REST, LANES), buf(4, REST, LANES),

time: 86.5 us -> 85.6 us (0.990)
  Pallas kernels: 85.7 us -> 84.8 us
where the time goes in v6:
time: 85.6 us; the launch traced here: 85.5 us
  Pallas kernels  84.8 us (99%)
    pallas_call x1, Pallas kernels, per_device(): pl.pallas_call(kernel, out_shape=(pltpu.VMEM((1, 128, 12288), BF16), pltp...  82.5 us
    pallas_call x1, Pallas kernels, per_device(): pl.pallas_call(finish, out_shape=(shape(1, 128, 12288, dtype=BF16), shape...  2.34 us

profile of v6, /device:TPU:1, one launch (start us, length us, event | category | flops | bytes accessed | tf_op | source)
XLA Modules:
  0.0 85.5 jit_solution(13578440204208343876)
XLA Ops:
  0.6 82.5 %hyena.1 = (bf16[1,128,12288]{2,1,0:T(8,128)(2,1)S(1)}, f32[88,128]{1,0:T(8,128)S(1)}) custom-call(bf16[1,128,12288]{2,1,0:T(8,128)(2,1)} %rows_hbm.1, bf16[1,128,4096]{2,1,0:T(8,128)(2,1)} %cot_hbm.1, f32[3,768]{1,0:T(4,128)} %taps.1, f32[16,256]{1,0:T(8,128)} %residues.1, f32[16,256]{1,0:T(8,128)} %rates.1, f32[1,256]{1,0:T(1,128)} %bitcast.2, ...), custom_call_target="tpu_custom_call" | custom-call | flops 100000000 | bytes 8388608 | tf_op jit(solution)/shard_map/hyena/pallas_call | solution.py:670
  83.1 2.3 %finish.1 = (bf16[1,128,12288]{2,1,0:T(8,128)(2,1)}, f32[3,768]{1,0:T(4,128)}, f32[16,256]{1,0:T(8,128)}, f32[16,256]{1,0:T(8,128)}, f32[1,256]{1,0:T(1,128)}) custom-call(bf16[1,128,12288]{2,1,0:T(8,128)(2,1)S(1)} %get-tuple-element.12.rows_in, f32[88,128]{1,0:T(8,128)S(1)} %get-tuple-element.13.mine), custom_call_target="tpu_custom_call" | custom-call | tf_op jit(solution)/shard_map/finish/pallas_call | solution.py:698
